TPU v7x, 512 devices: a whole 4x4x16 slice. The times are simulated.
512 devices in a mesh: gx: 16 (over x, z_hi), gy: 32 (over y, z_lo, core).
Axes of the slice: x: 4, y: 4, z: 16 (z_hi: 4, z_lo: 4; z = z_hi * 4 + z_lo), core: 2. Of those that a mesh axis runs over, the one named last changes fastest.
Arguments:
- nest_wind: float32 [16, 1536, 6144], P(None, 'gy', 'gx'), may hold values from -6 to 6
- parent_wind: float32 [16, 512, 2048], P(None, 'gy', 'gx'), may hold values from -6 to 6
- diffusion: float32 [16], replicated, may hold values from 0.02 to 0.1
- drift: float32 [2, 16], replicated, may hold values from 0.05 to 0.3
- disk_sites: int32 [2, 32, 16, 8], P(None, 'gy', 'gx'), may hold values from 0 to 383, as said below
- disk_live: int32 [32, 16, 8], P('gy', 'gx'), may hold values from 0 to 1, as said below
- disk_coef: float32 [32, 16, 8], P('gy', 'gx'), may hold values from 0.05 to 0.3
Outputs:
- nest_out: float32 [16, 1536, 6144], P(None, 'gy', 'gx')
- parent_out: float32 [16, 512, 2048], P(None, 'gy', 'gx')
Inputs may be any that keep to these rules, and one draw needn't show every extreme that they name: `disk_sites`: row within 0 to 47 and column within 0 to 383 of the owner tile. `disk_live`: the live slots of a tile come first; every tile has one or more; in some rows of tiles every tile has all 8 slots live.
All inputs are finite; a program needn't handle non-finite values.
Results may differ from a plain program's by a relative error of at most 0.00011.
Values sent between devices are 32-bit elements; how exact they have to be, the bound alone decides.
A program may use at most 128 MiB of HBM per device.

v0:
```python
import jax
import jax.numpy as jnp
from jax import lax
from jax.sharding import PartitionSpec as P

FOOT = 6


SIGMA = 2.0
HIGH = lax.Precision.HIGHEST
FAR_AWAY = 1000000


def extended_2(array, sides, width):
    for axis, dim in sides:
        size, length = (lax.axis_size(axis), array.shape[dim])
        up = [(i, (i + 1) % size) for i in range(size - 1)]
        down = [(j, i) for i, j in up]
        last = lax.slice_in_dim(array, length - width, length, axis=dim)
        leading = lax.slice_in_dim(array, 0, width, axis=dim)
        before = lax.ppermute(last, axis, up)
        after = lax.ppermute(leading, axis, down)
        array = jnp.concatenate([before, array, after], axis=dim)
    return array


def shifted(block, axis, distance):
    devices = range(lax.axis_size(axis))
    route = [(i - distance, i) for i in devices if i - distance in devices]
    return lax.ppermute(block, axis, route)


def advance(padded, diffuse, drift):
    centre = padded[:, 1:-1, 1:-1]
    west = padded[:, 1:-1, :-2]
    east = padded[:, 1:-1, 2:]
    south = padded[:, :-2, 1:-1]
    north = padded[:, 2:, 1:-1]
    spread = east + west + north + south - 4.0 * centre
    return (
        centre
        + diffuse[:, None, None] * spread
        - drift[0][:, None, None] * (centre - west)
        - drift[1][:, None, None] * (centre - south)
    )


def weights(count):
    cells = jnp.arange(count, dtype=jnp.int32)
    coarse = cells // 3
    rest = cells % 3
    slots = jnp.arange(count // 3 + 2, dtype=jnp.int32)
    lower = jnp.where(rest == 0, 1.0 / 3.0, 0.0)
    middle = jnp.where(rest == 1, 1.0, 2.0 / 3.0)
    upper = jnp.where(rest == 2, 1.0 / 3.0, 0.0)
    table = (
        lower[:, None] * (slots[None, :] == coarse[:, None])
        + middle[:, None] * (slots[None, :] == coarse[:, None] + 1)
        + upper[:, None] * (slots[None, :] == coarse[:, None] + 2)
    )
    return table.astype(jnp.float32)


def interpolate(padded, row_table, col_table):
    first = jnp.einsum("cmn,xn->cmx", padded, col_table, precision=HIGH)
    return jnp.einsum("ym,cmx->cyx", row_table, first, precision=HIGH)


def footprint(offset):
    inside = jnp.abs(offset) <= FOOT
    value = jnp.exp(-(offset * offset) / (2.0 * SIGMA * SIGMA))
    return jnp.where(inside, value, 0.0)


def thrust(nest, rows, cols, live, coef):
    levels = nest.shape[0] // 2
    east_part = nest[:levels, rows, cols]
    north_part = nest[levels:, rows, cols]
    speed = jnp.sqrt(east_part * east_part + north_part * north_part + 1.0)
    scale = -(coef * live)
    return jnp.concatenate([scale * east_part * speed, scale * north_part * speed], axis=0)


def parent_rims(field):
    return extended_2(field, (("gx", 2), ("gy", 1)), 1)


def spread_force(amounts, rows, cols, rows_n, cols_n):
    chans = amounts.shape[0]
    span_rows = jnp.concatenate(
        [jnp.arange(rows_n + FOOT, dtype=jnp.int32), jnp.arange(-FOOT, 0, dtype=jnp.int32)]
    )
    filler = jnp.full((128 - 2 * FOOT,), FAR_AWAY, jnp.int32)
    span_cols = jnp.concatenate(
        [jnp.arange(cols_n + FOOT, dtype=jnp.int32), jnp.arange(-FOOT, 0, dtype=jnp.int32), filler]
    )
    row_prof = footprint((span_rows[:, None] - rows[None, :]).astype(jnp.float32))
    col_prof = footprint((span_cols[:, None] - cols[None, :]).astype(jnp.float32))
    scaled = (amounts[:, None, :] * row_prof[None]).reshape(chans * (rows_n + 2 * FOOT), -1)
    wide = jnp.dot(scaled, col_prof.T, precision=HIGH).reshape(
        chans, rows_n + 2 * FOOT, cols_n + 128
    )
    spill_cols = wide[:, :, cols_n:]
    from_west = shifted(spill_cols, "gx", 1)
    from_east = shifted(spill_cols, "gx", -1)
    middle = (
        wide[:, :, :cols_n]
        + jnp.pad(from_west[:, :, :FOOT], ((0, 0), (0, 0), (0, cols_n - FOOT)))
        + jnp.pad(from_east[:, :, FOOT : 2 * FOOT], ((0, 0), (0, 0), (cols_n - FOOT, 0)))
    )
    from_south = shifted(middle[:, rows_n : rows_n + FOOT], "gy", 1)
    from_north = shifted(middle[:, rows_n + FOOT :], "gy", -1)
    return (
        middle[:, :rows_n]
        + jnp.pad(from_south, ((0, 0), (0, rows_n - FOOT), (0, 0)))
        + jnp.pad(from_north, ((0, 0), (rows_n - FOOT, 0), (0, 0)))
    )


def smooth(padded):
    across = (padded[:, :, :-2] + 2.0 * padded[:, :, 1:-1] + padded[:, :, 2:]) * 0.25
    return (across[:, :-2] + 2.0 * across[:, 1:-1] + across[:, 2:]) * 0.25


def on_device(nest_wind, parent_wind, diffusion, drift, disk_sites, disk_live, disk_coef):
    chans, rows_n, cols_n = nest_wind.shape
    prow = parent_wind.shape[1]
    pcol = parent_wind.shape[2]
    row_pos = lax.axis_index("gy")
    col_pos = lax.axis_index("gx")
    tiles_y = lax.axis_size("gy")
    tiles_x = lax.axis_size("gx")
    old_ext = parent_rims(parent_wind)
    parent_new = advance(old_ext, diffusion / 3.0, drift)
    new_ext = parent_rims(parent_new)
    row_table = weights(rows_n)
    col_table = weights(cols_n)
    bound_old = interpolate(old_ext, row_table, col_table)
    bound_new = interpolate(new_ext, row_table, col_table)
    glob_rows = row_pos * rows_n + jnp.arange(rows_n, dtype=jnp.int32)
    glob_cols = col_pos * cols_n + jnp.arange(cols_n, dtype=jnp.int32)
    cycle = ((glob_rows == 0) | (glob_rows == rows_n * tiles_y - 1))[:, None] | (
        (glob_cols == 0) | (glob_cols == cols_n * tiles_x - 1)
    )[None, :]
    rows = disk_sites[0, 0, 0]
    cols = disk_sites[1, 0, 0]
    live = disk_live[0, 0].astype(jnp.float32)
    coef = disk_coef[0, 0]
    nest = nest_wind
    for step in range(1, 4):
        amounts = thrust(nest, rows, cols, live, coef)
        force = spread_force(amounts, rows, cols, rows_n, cols_n)
        extended = extended_2(nest, (("gx", 2), ("gy", 1)), 1)
        stepped = advance(extended, diffusion, drift) + force
        bound = bound_old + step / 3.0 * (bound_new - bound_old)
        nest = jnp.where(cycle[None], bound, stepped)
    average = nest.reshape(chans, prow, 3, pcol, 3).mean(axis=(2, 4))
    mixed = parent_new + 0.5 * (average - parent_new)
    mixed_ext = extended_2(mixed, (("gx", 2), ("gy", 1)), 1)
    return (nest, smooth(mixed_ext))


def solution(mesh):
    placed = (
        P(None, "gy", "gx"),
        P(None, "gy", "gx"),
        P(),
        P(),
        P(None, "gy", "gx", None),
        P("gy", "gx", None),
        P("gy", "gx", None),
    )
    return jax.shard_map(
        on_device,
        mesh=mesh,
        in_specs=placed,
        out_specs=(P(None, "gy", "gx"), P(None, "gy", "gx")),
        check_vma=False,
    )
```

profile of v0, /device:TPU:109, one launch (start us, length us, event | category | flops | bytes accessed | tf_op | source)
XLA Modules:
  0.0 653.4 jit_solution(15469078033543868061)
XLA Ops:
  2.0 7.0 %copy.28 = f32[16,48,384]{0,2,1:T(8,128)} copy(f32[16,48,384]{2,1,0:T(8,128)} %param.7) | data formatting | bytes 2359296
  9.1 26.6 %while.7 = (s32[]{:T(128)}, f32[16,48,384]{0,2,1:T(8,128)}, s32[8,3]{0,1:T(4,128)S(1)}, f32[8,8]{1,0:T(8,128)S(1)}, s32[]{:T(128)}, /*index=5*/s32[]{:T(128)}) while((s32[]{:T(128)}, f32[16,48,384]{0,2,1:T(8,128)}, s32[8,3]{0,1:T(4,128)S(1)}, f32[8,8]{1,0:T(8,128)S(1)}, s32[]{:T(128)}, /*index=5*/s32[]{:T(128)}) %tuple.147), condition=%wide.while_cond.1, body=%wide.while_body.1.sunk | while | flops 2 | bytes 265 | solution.py:78
  35.7 26.9 %while.6 = (s32[]{:T(128)}, f32[16,48,384]{0,2,1:T(8,128)}, s32[8,3]{0,1:T(4,128)S(1)}, f32[8,8]{1,0:T(8,128)S(1)}, s32[]{:T(128)}, /*index=5*/s32[]{:T(128)}) while((s32[]{:T(128)}, f32[16,48,384]{0,2,1:T(8,128)}, s32[8,3]{0,1:T(4,128)S(1)}, f32[8,8]{1,0:T(8,128)S(1)}, s32[]{:T(128)}, /*index=5*/s32[]{:T(128)}) %tuple.162), condition=%wide.while_cond, body=%wide.while_body.sunk | while | flops 2 | bytes 265 | solution.py:77
  66.1 9.8 %collective-permute-start.13 = (f32[16,60,128]{2,1,0:T(8,128)}, f32[16,60,128]{2,1,0:T(8,128)}, u32[]{:S(2)}, u32[]{:S(2)}) collective-permute-start(f32[16,60,128]{2,1,0:T(8,128)} %slice.387), channel_id=1, source_target_pairs={{32,0},{64,32},{96,64},{128,96},{160,128},{192,160},{224,192},{256... | collective-permute-start | bytes 1474568 | tf_op jit(solution)/shard_map/ppermute | solution.py:30
  78.7 6.3 collective-permute-start
  85.0 3.8 collective-permute-start.1
  89.8 7.3 %collective-permute-start.8 = (f32[16,48,1]{2,1,0:T(8,128)}, f32[16,48,1]{2,1,0:T(8,128)}, u32[]{:S(2)}, u32[]{:S(2)}) collective-permute-start(f32[16,48,1]{2,1,0:T(8,128)} %get-tuple-element.205), channel_id=1, source_target_pairs={{32,0},{64,32},{96,64},{128,96},{160,128},{192,160},{224,192},{256... | collective-permute-start | bytes 9224 | tf_op jit(solution)/shard_map/ppermute | solution.py:22
  104.8 36.6 %collective-permute-done = f32[16,16,1]{2,1,0:T(8,128)S(1)} collective-permute-done((f32[16,16,1]{2,1,0:T(8,128)}, f32[16,16,1]{2,1,0:T(8,128)S(1)}, u32[]{:S(2)}, u32[]{:S(2)}) %collective-permute-start) | collective-permute-done | bytes 1056 | tf_op jit(solution)/shard_map/ppermute | solution.py:21
  144.4 17.9 %collective-permute-start.2 = (f32[16,1,130]{2,1,0:T(1,128)S(1)}, f32[16,1,130]{2,1,0:T(1,128)S(1)}, u32[]{:S(2)}, u32[]{:S(2)}) collective-permute-start(f32[16,1,130]{2,1,0:T(1,128)S(1)} %get-tuple-element.210), channel_id=1, source_target_pairs={{0,1},{1,2},{2,3},{3,4},{4,5},{5,6},{6,7},{7,8},{8,9},{9,10},{10,1... | collective-permute-start | bytes 24968 | tf_op jit(solution)/shard_map/ppermute | solution.py:21
  165.2 9.9 %collective-permute-done.9 = f32[16,48,1]{2,1,0:T(8,128)S(1)} collective-permute-done((f32[16,48,1]{2,1,0:T(8,128)}, f32[16,48,1]{2,1,0:T(8,128)S(1)}, u32[]{:S(2)}, u32[]{:S(2)}) %collective-permute-start.9) | collective-permute-done | bytes 3104 | tf_op jit(solution)/shard_map/ppermute | solution.py:21
  180.3 7.0 %collective-permute-start.4 = (f32[16,16,1]{2,1,0:T(8,128)S(1)}, f32[16,16,1]{2,1,0:T(8,128)S(1)}, u32[]{:S(2)}, u32[]{:S(2)}) collective-permute-start(f32[16,16,1]{2,1,0:T(8,128)S(1)} %get-tuple-element.214), channel_id=1, source_target_pairs={{0,32},{32,64},{64,96},{96,128},{128,160},{160,192},{192,224},{224... | collective-permute-start | bytes 3080 | tf_op jit(solution)/shard_map/ppermute | solution.py:21
  187.3 3.0 collective-permute-start.5
  193.5 7.3 %collective-permute-start.11 = (f32[16,1,386]{2,1,0:T(1,128)S(1)}, f32[16,1,386]{2,1,0:T(1,128)S(1)}, u32[]{:S(2)}, u32[]{:S(2)}) collective-permute-start(f32[16,1,386]{2,1,0:T(1,128)S(1)} %get-tuple-element.192), channel_id=1, source_target_pairs={{0,1},{1,2},{2,3},{3,4},{4,5},{5,6},{6,7},{7,8},{8,9},{9,10},{10,1... | collective-permute-start | bytes 74120 | tf_op jit(solution)/shard_map/ppermute | solution.py:21
  209.1 6.4 collective-permute-start.14
  219.1 6.1 collective-permute-done.15
  225.2 4.0 fusion.32
  229.2 5.6 copy.31
  234.9 25.9 %while.9 = (s32[]{:T(128)}, f32[16,48,384]{0,2,1:T(8,128)}, s32[8,3]{0,1:T(4,128)S(1)}, f32[8,8]{1,0:T(8,128)S(1)}, s32[]{:T(128)}, /*index=5*/s32[]{:T(128)}) while((s32[]{:T(128)}, f32[16,48,384]{0,2,1:T(8,128)}, s32[8,3]{0,1:T(4,128)S(1)}, f32[8,8]{1,0:T(8,128)S(1)}, s32[]{:T(128)}, /*index=5*/s32[]{:T(128)}) %tuple.167), condition=%wide.while_cond.3, body=%wide.while_body.3.sunk | while | flops 2 | bytes 265 | solution.py:78
  260.8 26.6 %while.8 = (s32[]{:T(128)}, f32[16,48,384]{0,2,1:T(8,128)}, s32[8,3]{0,1:T(4,128)S(1)}, f32[8,8]{1,0:T(8,128)S(1)}, s32[]{:T(128)}, /*index=5*/s32[]{:T(128)}) while((s32[]{:T(128)}, f32[16,48,384]{0,2,1:T(8,128)}, s32[8,3]{0,1:T(4,128)S(1)}, f32[8,8]{1,0:T(8,128)S(1)}, s32[]{:T(128)}, /*index=5*/s32[]{:T(128)}) %tuple.165), condition=%wide.while_cond.2, body=%wide.while_body.2.sunk | while | flops 2 | bytes 265 | solution.py:77
  289.8 3.8 collective-permute-start.21
  293.6 5.4 collective-permute-start.20
  299.0 36.5 %collective-permute-done.21 = f32[16,60,128]{2,1,0:T(8,128)S(1)} collective-permute-done((f32[16,60,128]{2,1,0:T(8,128)S(1)}, f32[16,60,128]{2,1,0:T(8,128)S(1)}, u32[]{:S(2)}, u32[]{:S(2)}) %collective-permute-start.21) | collective-permute-done | bytes 491552 | tf_op jit(solution)/shard_map/ppermute | solution.py:30
  335.7 3.8 collective-permute-done.20
  340.6 6.2 collective-permute-start.22
  348.9 7.6 %collective-permute-start.16 = (f32[16,48,1]{2,1,0:T(8,128)S(1)}, f32[16,48,1]{2,1,0:T(8,128)S(1)}, u32[]{:S(2)}, u32[]{:S(2)}) collective-permute-start(f32[16,48,1]{2,1,0:T(8,128)S(1)} %get-tuple-element.203), channel_id=1, source_target_pairs={{32,0},{64,32},{96,64},{128,96},{160,128},{192,160},{224,192},{256... | collective-permute-start | bytes 9224 | tf_op jit(solution)/shard_map/ppermute | solution.py:22
  358.5 20.8 %collective-permute-done.16 = f32[16,48,1]{2,1,0:T(8,128)S(1)} collective-permute-done((f32[16,48,1]{2,1,0:T(8,128)S(1)}, f32[16,48,1]{2,1,0:T(8,128)S(1)}, u32[]{:S(2)}, u32[]{:S(2)}) %collective-permute-start.16) | collective-permute-done | bytes 3104 | tf_op jit(solution)/shard_map/ppermute | solution.py:22
  379.3 7.7 %collective-permute-done.17 = f32[16,48,1]{2,1,0:T(8,128)S(1)} collective-permute-done((f32[16,48,1]{2,1,0:T(8,128)S(1)}, f32[16,48,1]{2,1,0:T(8,128)S(1)}, u32[]{:S(2)}, u32[]{:S(2)}) %collective-permute-start.17) | collective-permute-done | bytes 3104 | tf_op jit(solution)/shard_map/ppermute | solution.py:21
  389.7 8.9 %collective-permute-start.19 = (f32[16,1,386]{2,1,0:T(1,128)S(1)}, f32[16,1,386]{2,1,0:T(1,128)S(1)}, u32[]{:S(2)}, u32[]{:S(2)}) collective-permute-start(f32[16,1,386]{2,1,0:T(1,128)S(1)} %get-tuple-element.190), channel_id=1, source_target_pairs={{0,1},{1,2},{2,3},{3,4},{4,5},{5,6},{6,7},{7,8},{8,9},{9,10},{10,1... | collective-permute-start | bytes 74120 | tf_op jit(solution)/shard_map/ppermute | solution.py:21
  400.9 3.8 fusion.19
  404.8 5.6 copy.34
  410.4 25.9 %while.11 = (s32[]{:T(128)}, f32[16,48,384]{0,2,1:T(8,128)}, s32[8,3]{0,1:T(4,128)S(1)}, f32[8,8]{1,0:T(8,128)S(1)}, s32[]{:T(128)}, /*index=5*/s32[]{:T(128)}) while((s32[]{:T(128)}, f32[16,48,384]{0,2,1:T(8,128)}, s32[8,3]{0,1:T(4,128)S(1)}, f32[8,8]{1,0:T(8,128)S(1)}, s32[]{:T(128)}, /*index=5*/s32[]{:T(128)}) %tuple.168), condition=%wide.while_cond.5, body=%wide.while_body.5.sunk | while | flops 2 | bytes 265 | solution.py:78
  436.3 26.6 %while.10 = (s32[]{:T(128)}, f32[16,48,384]{0,2,1:T(8,128)}, s32[8,3]{0,1:T(4,128)S(1)}, f32[8,8]{1,0:T(8,128)S(1)}, s32[]{:T(128)}, /*index=5*/s32[]{:T(128)}) while((s32[]{:T(128)}, f32[16,48,384]{0,2,1:T(8,128)}, s32[8,3]{0,1:T(4,128)S(1)}, f32[8,8]{1,0:T(8,128)S(1)}, s32[]{:T(128)}, /*index=5*/s32[]{:T(128)}) %tuple.166), condition=%wide.while_cond.4, body=%wide.while_body.4.sunk | while | flops 2 | bytes 265 | solution.py:77
  465.3 5.7 collective-permute-start.29
  471.0 3.5 collective-permute-start.28
  474.5 29.2 %collective-permute-done.29 = f32[16,60,128]{2,1,0:T(8,128)S(1)} collective-permute-done((f32[16,60,128]{2,1,0:T(8,128)S(1)}, f32[16,60,128]{2,1,0:T(8,128)S(1)}, u32[]{:S(2)}, u32[]{:S(2)}) %collective-permute-start.29) | collective-permute-done | bytes 491552 | tf_op jit(solution)/shard_map/ppermute | solution.py:30
  503.9 19.6 %collective-permute-done.28 = f32[16,60,128]{2,1,0:T(8,128)S(1)} collective-permute-done((f32[16,60,128]{2,1,0:T(8,128)S(1)}, f32[16,60,128]{2,1,0:T(8,128)S(1)}, u32[]{:S(2)}, u32[]{:S(2)}) %collective-permute-start.28) | collective-permute-done | bytes 491552 | tf_op jit(solution)/shard_map/ppermute | solution.py:30
  530.9 7.3 %collective-permute-start.25 = (f32[16,48,1]{2,1,0:T(8,128)S(1)}, f32[16,48,1]{2,1,0:T(8,128)S(1)}, u32[]{:S(2)}, u32[]{:S(2)}) collective-permute-start(f32[16,48,1]{2,1,0:T(8,128)S(1)} %get-tuple-element.200), channel_id=1, source_target_pairs={{0,32},{32,64},{64,96},{96,128},{128,160},{160,192},{192,224},{224... | collective-permute-start | bytes 9224 | tf_op jit(solution)/shard_map/ppermute | solution.py:21
  538.2 24.4 %collective-permute-done.24 = f32[16,48,1]{2,1,0:T(8,128)S(1)} collective-permute-done((f32[16,48,1]{2,1,0:T(8,128)S(1)}, f32[16,48,1]{2,1,0:T(8,128)S(1)}, u32[]{:S(2)}, u32[]{:S(2)}) %collective-permute-start.24) | collective-permute-done | bytes 3104 | tf_op jit(solution)/shard_map/ppermute | solution.py:22
  562.6 8.7 %collective-permute-done.25 = f32[16,48,1]{2,1,0:T(8,128)S(1)} collective-permute-done((f32[16,48,1]{2,1,0:T(8,128)S(1)}, f32[16,48,1]{2,1,0:T(8,128)S(1)}, u32[]{:S(2)}, u32[]{:S(2)}) %collective-permute-start.25) | collective-permute-done | bytes 3104 | tf_op jit(solution)/shard_map/ppermute | solution.py:21
  574.2 8.1 %collective-permute-start.27 = (f32[16,1,386]{2,1,0:T(1,128)S(1)}, f32[16,1,386]{2,1,0:T(1,128)S(1)}, u32[]{:S(2)}, u32[]{:S(2)}) collective-permute-start(f32[16,1,386]{2,1,0:T(1,128)S(1)} %get-tuple-element.188), channel_id=1, source_target_pairs={{0,1},{1,2},{2,3},{3,4},{4,5},{5,6},{6,7},{7,8},{8,9},{9,10},{10,1... | collective-permute-start | bytes 74120 | tf_op jit(solution)/shard_map/ppermute | solution.py:21
  586.0 7.0 %copy.37 = f32[16,48,384]{0,2,1:T(8,128)} copy(f32[16,48,384]{2,1,0:T(8,128)} %fusion.6) | data formatting | bytes 2359296 | tf_op jit(solution)/shard_map/jit(_where)/select_n | solution.py:156
  593.0 15.0 %reshape.254 = f32[16,16,3,128,3]{0,4,3,2,1:T(4,128)} reshape(f32[16,48,384]{0,2,1:T(8,128)} %copy.37) | data formatting | bytes 2359296 | tf_op jit(solution)/shard_map/reshape | solution.py:157
  608.0 9.1 %reduce_sum.9 = f32[16,16,128]{0,2,1:T(8,128)S(1)} reduce(f32[16,16,3,128,3]{0,4,3,2,1:T(4,128)} %reshape.254, f32[]{:T(128)} %constant.42.clone.1), dimensions={2,4}, to_apply=%region_0.1 | reduce | flops 262144 | bytes 1310724 | tf_op jit(solution)/shard_map/reduce_sum | solution.py:157
  621.6 7.9 %collective-permute-start.33 = (f32[16,16,1]{2,1,0:T(8,128)S(1)}, f32[16,16,1]{2,1,0:T(8,128)S(1)}, u32[]{:S(2)}, u32[]{:S(2)}) collective-permute-start(f32[16,16,1]{2,1,0:T(8,128)S(1)} %get-tuple-element.213), channel_id=1, source_target_pairs={{32,0},{64,32},{96,64},{128,96},{160,128},{192,160},{224,192},{256... | collective-permute-start | bytes 3080 | tf_op jit(solution)/shard_map/ppermute | solution.py:22
  629.5 3.9 collective-permute-done.32
  633.3 3.4 collective-permute-done.33
  636.9 7.6 %collective-permute-start.34 = (f32[16,1,130]{2,1,0:T(1,128)S(1)}, f32[16,1,130]{2,1,0:T(1,128)S(1)}, u32[]{:S(2)}, u32[]{:S(2)}) collective-permute-start(f32[16,1,130]{2,1,0:T(1,128)S(1)} %get-tuple-element.206), channel_id=1, source_target_pairs={{0,1},{1,2},{2,3},{3,4},{4,5},{5,6},{6,7},{7,8},{8,9},{9,10},{10,1... | collective-permute-start | bytes 24968 | tf_op jit(solution)/shard_map/ppermute | solution.py:21
  646.5 5.8 collective-permute-done.35
  (408 shorter events, 236.9 us)
Async XLA Ops:
  2.0 61.1 %copy-start.24 = (s32[8]{0:T(128)}, s32[8]{0:T(128)S(1)}, u32[]{:S(2)}) copy-start(s32[8]{0:T(128)S(1)} %get-tuple-element.226) | copy-start | bytes 100
  2.0 60.6 %copy-start.48 = (f32[1,1,8]{2,1,0:T(1,128)S(1)}, f32[1,1,8]{2,1,0:T(1,128)}, u32[]{:S(2)}) copy-start(f32[1,1,8]{2,1,0:T(1,128)} %param.13) | copy-start | bytes 100
  2.0 60.6 %copy-start.49 = (s32[1,1,8]{2,1,0:T(1,128)S(1)}, s32[1,1,8]{2,1,0:T(1,128)}, u32[]{:S(2)}) copy-start(s32[1,1,8]{2,1,0:T(1,128)} %param.12) | copy-start | bytes 100
  66.1 138.3 %collective-permute-start.13 = (f32[16,60,128]{2,1,0:T(8,128)}, f32[16,60,128]{2,1,0:T(8,128)}, u32[]{:S(2)}, u32[]{:S(2)}) collective-permute-start(f32[16,60,128]{2,1,0:T(8,128)} %slice.387), channel_id=1, source_target_pairs={{32,0},{64,32},{96,64},{128,96},{160,128},{192,160},{224,192},{256... | collective-permute-start | bytes 1474568 | tf_op jit(solution)/shard_map/ppermute | solution.py:30
  76.0 131.7 %collective-permute-start.12 = (f32[16,60,128]{2,1,0:T(8,128)}, f32[16,60,128]{2,1,0:T(8,128)}, u32[]{:S(2)}, u32[]{:S(2)}) collective-permute-start(f32[16,60,128]{2,1,0:T(8,128)} %slice.387), channel_id=1, source_target_pairs={{0,32},{32,64},{64,96},{96,128},{128,160},{160,192},{192,224},{224... | collective-permute-start | bytes 1474568 | tf_op jit(solution)/shard_map/ppermute | solution.py:30
  78.7 62.7 %collective-permute-start = (f32[16,16,1]{2,1,0:T(8,128)}, f32[16,16,1]{2,1,0:T(8,128)S(1)}, u32[]{:S(2)}, u32[]{:S(2)}) collective-permute-start(f32[16,16,1]{2,1,0:T(8,128)} %get-tuple-element.216), channel_id=1, source_target_pairs={{0,32},{32,64},{64,96},{96,128},{128,160},{160,192},{192,224},{224... | collective-permute-start | bytes 3080 | tf_op jit(solution)/shard_map/ppermute | solution.py:21
  85.0 58.4 %collective-permute-start.1 = (f32[16,16,1]{2,1,0:T(8,128)}, f32[16,16,1]{2,1,0:T(8,128)}, u32[]{:S(2)}, u32[]{:S(2)}) collective-permute-start(f32[16,16,1]{2,1,0:T(8,128)} %get-tuple-element.217), channel_id=1, source_target_pairs={{32,0},{64,32},{96,64},{128,96},{160,128},{192,160},{224,192},{256... | collective-permute-start | bytes 3080 | tf_op jit(solution)/shard_map/ppermute | solution.py:22
  89.8 72.5 %collective-permute-start.8 = (f32[16,48,1]{2,1,0:T(8,128)}, f32[16,48,1]{2,1,0:T(8,128)}, u32[]{:S(2)}, u32[]{:S(2)}) collective-permute-start(f32[16,48,1]{2,1,0:T(8,128)} %get-tuple-element.205), channel_id=1, source_target_pairs={{32,0},{64,32},{96,64},{128,96},{160,128},{192,160},{224,192},{256... | collective-permute-start | bytes 9224 | tf_op jit(solution)/shard_map/ppermute | solution.py:22
  141.4 33.7 %collective-permute-start.9 = (f32[16,48,1]{2,1,0:T(8,128)}, f32[16,48,1]{2,1,0:T(8,128)S(1)}, u32[]{:S(2)}, u32[]{:S(2)}) collective-permute-start(f32[16,48,1]{2,1,0:T(8,128)} %get-tuple-element.204), channel_id=1, source_target_pairs={{0,32},{32,64},{64,96},{96,128},{128,160},{160,192},{192,224},{224... | collective-permute-start | bytes 9224 | tf_op jit(solution)/shard_map/ppermute | solution.py:21
  144.4 34.3 %collective-permute-start.2 = (f32[16,1,130]{2,1,0:T(1,128)S(1)}, f32[16,1,130]{2,1,0:T(1,128)S(1)}, u32[]{:S(2)}, u32[]{:S(2)}) collective-permute-start(f32[16,1,130]{2,1,0:T(1,128)S(1)} %get-tuple-element.210), channel_id=1, source_target_pairs={{0,1},{1,2},{2,3},{3,4},{4,5},{5,6},{6,7},{7,8},{8,9},{9,10},{10,1... | collective-permute-start | bytes 24968 | tf_op jit(solution)/shard_map/ppermute | solution.py:21
  162.4 16.4 %collective-permute-start.3 = (f32[16,1,130]{2,1,0:T(1,128)S(1)}, f32[16,1,130]{2,1,0:T(1,128)S(1)}, u32[]{:S(2)}, u32[]{:S(2)}) collective-permute-start(f32[16,1,130]{2,1,0:T(1,128)S(1)} %get-tuple-element.211), channel_id=1, source_target_pairs={{1,0},{2,1},{3,2},{4,3},{5,4},{6,5},{7,6},{8,7},{9,8},{10,9},{11,1... | collective-permute-start | bytes 24968 | tf_op jit(solution)/shard_map/ppermute | solution.py:22
  176.2 42.4 %collective-permute-start.10 = (f32[16,1,386]{2,1,0:T(1,128)S(1)}, f32[16,1,386]{2,1,0:T(1,128)S(1)}, u32[]{:S(2)}, u32[]{:S(2)}) collective-permute-start(f32[16,1,386]{2,1,0:T(1,128)S(1)} %get-tuple-element.193), channel_id=1, source_target_pairs={{1,0},{2,1},{3,2},{4,3},{5,4},{6,5},{7,6},{8,7},{9,8},{10,9},{11,1... | collective-permute-start | bytes 74120 | tf_op jit(solution)/shard_map/ppermute | solution.py:22
  180.3 13.2 %collective-permute-start.4 = (f32[16,16,1]{2,1,0:T(8,128)S(1)}, f32[16,16,1]{2,1,0:T(8,128)S(1)}, u32[]{:S(2)}, u32[]{:S(2)}) collective-permute-start(f32[16,16,1]{2,1,0:T(8,128)S(1)} %get-tuple-element.214), channel_id=1, source_target_pairs={{0,32},{32,64},{64,96},{96,128},{128,160},{160,192},{192,224},{224... | collective-permute-start | bytes 3080 | tf_op jit(solution)/shard_map/ppermute | solution.py:21
  187.3 14.6 %collective-permute-start.5 = (f32[16,16,1]{2,1,0:T(8,128)S(1)}, f32[16,16,1]{2,1,0:T(8,128)S(1)}, u32[]{:S(2)}, u32[]{:S(2)}) collective-permute-start(f32[16,16,1]{2,1,0:T(8,128)S(1)} %get-tuple-element.215), channel_id=1, source_target_pairs={{32,0},{64,32},{96,64},{128,96},{160,128},{192,160},{224,192},{256... | collective-permute-start | bytes 3080 | tf_op jit(solution)/shard_map/ppermute | solution.py:22
  193.5 25.1 %collective-permute-start.11 = (f32[16,1,386]{2,1,0:T(1,128)S(1)}, f32[16,1,386]{2,1,0:T(1,128)S(1)}, u32[]{:S(2)}, u32[]{:S(2)}) collective-permute-start(f32[16,1,386]{2,1,0:T(1,128)S(1)} %get-tuple-element.192), channel_id=1, source_target_pairs={{0,1},{1,2},{2,3},{3,4},{4,5},{5,6},{6,7},{7,8},{8,9},{9,10},{10,1... | collective-permute-start | bytes 74120 | tf_op jit(solution)/shard_map/ppermute | solution.py:21
  202.1 13.4 %collective-permute-start.6 = (f32[16,1,130]{2,1,0:T(1,128)S(1)}, f32[16,1,130]{2,1,0:T(1,128)S(1)}, u32[]{:S(2)}, u32[]{:S(2)}) collective-permute-start(f32[16,1,130]{2,1,0:T(1,128)S(1)} %get-tuple-element.208), channel_id=1, source_target_pairs={{0,1},{1,2},{2,3},{3,4},{4,5},{5,6},{6,7},{7,8},{8,9},{9,10},{10,1... | collective-permute-start | bytes 24968 | tf_op jit(solution)/shard_map/ppermute | solution.py:21
  204.4 13.2 %collective-permute-start.7 = (f32[16,1,130]{2,1,0:T(1,128)S(1)}, f32[16,1,130]{2,1,0:T(1,128)S(1)}, u32[]{:S(2)}, u32[]{:S(2)}) collective-permute-start(f32[16,1,130]{2,1,0:T(1,128)S(1)} %get-tuple-element.209), channel_id=1, source_target_pairs={{1,0},{2,1},{3,2},{4,3},{5,4},{6,5},{7,6},{8,7},{9,8},{10,9},{11,1... | collective-permute-start | bytes 24968 | tf_op jit(solution)/shard_map/ppermute | solution.py:22
  209.1 10.0 %collective-permute-start.14 = (f32[16,6,384]{2,1,0:T(8,128)S(1)}, f32[16,6,384]{2,1,0:T(8,128)S(1)}, u32[]{:S(2)}, u32[]{:S(2)}) collective-permute-start(f32[16,6,384]{2,1,0:T(8,128)S(1)} %get-tuple-element.198), channel_id=1, source_target_pairs={{0,1},{1,2},{2,3},{3,4},{4,5},{5,6},{6,7},{7,8},{8,9},{9,10},{10,1... | collective-permute-start | bytes 442376 | tf_op jit(solution)/shard_map/ppermute | solution.py:30
  215.5 9.7 %collective-permute-start.15 = (f32[16,6,384]{2,1,0:T(8,128)S(1)}, f32[16,6,384]{2,1,0:T(8,128)S(1)}, u32[]{:S(2)}, u32[]{:S(2)}) collective-permute-start(f32[16,6,384]{2,1,0:T(8,128)S(1)} %get-tuple-element.199), channel_id=1, source_target_pairs={{1,0},{2,1},{3,2},{4,3},{5,4},{6,5},{7,6},{8,7},{9,8},{10,9},{11,1... | collective-permute-start | bytes 442376 | tf_op jit(solution)/shard_map/ppermute | solution.py:30
  229.2 58.1 %copy-start.28 = (f32[8]{0:T(128)S(1)}, f32[8]{0:T(128)}, u32[]{:S(2)}) copy-start(f32[8]{0:T(128)} %copy-done.27) | copy-start | bytes 100
  229.2 58.4 %copy-start.25 = (s32[8]{0:T(128)S(1)}, s32[8]{0:T(128)}, u32[]{:S(2)}) copy-start(s32[8]{0:T(128)} %copy-done.24) | copy-start | bytes 100
  289.8 45.7 %collective-permute-start.21 = (f32[16,60,128]{2,1,0:T(8,128)S(1)}, f32[16,60,128]{2,1,0:T(8,128)S(1)}, u32[]{:S(2)}, u32[]{:S(2)}) collective-permute-start(f32[16,60,128]{2,1,0:T(8,128)S(1)} %slice.396), channel_id=1, source_target_pairs={{32,0},{64,32},{96,64},{128,96},{160,128},{192,160},{224,192},{256... | collective-permute-start | bytes 1474568 | tf_op jit(solution)/shard_map/ppermute | solution.py:30
  293.6 45.9 %collective-permute-start.20 = (f32[16,60,128]{2,1,0:T(8,128)S(1)}, f32[16,60,128]{2,1,0:T(8,128)S(1)}, u32[]{:S(2)}, u32[]{:S(2)}) collective-permute-start(f32[16,60,128]{2,1,0:T(8,128)S(1)} %slice.396), channel_id=1, source_target_pairs={{0,32},{32,64},{64,96},{96,128},{128,160},{160,192},{192,224},{224... | collective-permute-start | bytes 1474568 | tf_op jit(solution)/shard_map/ppermute | solution.py:30
  340.6 58.9 %collective-permute-start.22 = (f32[16,6,384]{2,1,0:T(8,128)}, f32[16,6,384]{2,1,0:T(8,128)S(1)}, u32[]{:S(2)}, u32[]{:S(2)}) collective-permute-start(f32[16,6,384]{2,1,0:T(8,128)} %get-tuple-element.196), channel_id=1, source_target_pairs={{0,1},{1,2},{2,3},{3,4},{4,5},{5,6},{6,7},{7,8},{8,9},{9,10},{10,1... | collective-permute-start | bytes 442376 | tf_op jit(solution)/shard_map/ppermute | solution.py:30
  346.8 52.8 %collective-permute-start.23 = (f32[16,6,384]{2,1,0:T(8,128)}, f32[16,6,384]{2,1,0:T(8,128)S(1)}, u32[]{:S(2)}, u32[]{:S(2)}) collective-permute-start(f32[16,6,384]{2,1,0:T(8,128)} %get-tuple-element.197), channel_id=1, source_target_pairs={{1,0},{2,1},{3,2},{4,3},{5,4},{6,5},{7,6},{8,7},{9,8},{10,9},{11,1... | collective-permute-start | bytes 442376 | tf_op jit(solution)/shard_map/ppermute | solution.py:30
  348.9 30.4 %collective-permute-start.16 = (f32[16,48,1]{2,1,0:T(8,128)S(1)}, f32[16,48,1]{2,1,0:T(8,128)S(1)}, u32[]{:S(2)}, u32[]{:S(2)}) collective-permute-start(f32[16,48,1]{2,1,0:T(8,128)S(1)} %get-tuple-element.203), channel_id=1, source_target_pairs={{32,0},{64,32},{96,64},{128,96},{160,128},{192,160},{224,192},{256... | collective-permute-start | bytes 9224 | tf_op jit(solution)/shard_map/ppermute | solution.py:22
  356.6 30.5 %collective-permute-start.17 = (f32[16,48,1]{2,1,0:T(8,128)S(1)}, f32[16,48,1]{2,1,0:T(8,128)S(1)}, u32[]{:S(2)}, u32[]{:S(2)}) collective-permute-start(f32[16,48,1]{2,1,0:T(8,128)S(1)} %get-tuple-element.202), channel_id=1, source_target_pairs={{0,32},{32,64},{64,96},{96,128},{128,160},{160,192},{192,224},{224... | collective-permute-start | bytes 9224 | tf_op jit(solution)/shard_map/ppermute | solution.py:21
  387.8 10.8 %collective-permute-start.18 = (f32[16,1,386]{2,1,0:T(1,128)S(1)}, f32[16,1,386]{2,1,0:T(1,128)S(1)}, u32[]{:S(2)}, u32[]{:S(2)}) collective-permute-start(f32[16,1,386]{2,1,0:T(1,128)S(1)} %get-tuple-element.191), channel_id=1, source_target_pairs={{1,0},{2,1},{3,2},{4,3},{5,4},{6,5},{7,6},{8,7},{9,8},{10,9},{11,1... | collective-permute-start | bytes 74120 | tf_op jit(solution)/shard_map/ppermute | solution.py:22
  389.7 9.9 %collective-permute-start.19 = (f32[16,1,386]{2,1,0:T(1,128)S(1)}, f32[16,1,386]{2,1,0:T(1,128)S(1)}, u32[]{:S(2)}, u32[]{:S(2)}) collective-permute-start(f32[16,1,386]{2,1,0:T(1,128)S(1)} %get-tuple-element.190), channel_id=1, source_target_pairs={{0,1},{1,2},{2,3},{3,4},{4,5},{5,6},{6,7},{7,8},{8,9},{9,10},{10,1... | collective-permute-start | bytes 74120 | tf_op jit(solution)/shard_map/ppermute | solution.py:21
  404.7 58.2 %copy-start.29 = (f32[8]{0:T(128)S(1)}, f32[8]{0:T(128)}, u32[]{:S(2)}) copy-start(f32[8]{0:T(128)} %copy-done.27) | copy-start | bytes 100
  404.7 58.4 %copy-start.26 = (s32[8]{0:T(128)S(1)}, s32[8]{0:T(128)}, u32[]{:S(2)}) copy-start(s32[8]{0:T(128)} %copy-done.24) | copy-start | bytes 100
  465.3 38.4 %collective-permute-start.29 = (f32[16,60,128]{2,1,0:T(8,128)S(1)}, f32[16,60,128]{2,1,0:T(8,128)S(1)}, u32[]{:S(2)}, u32[]{:S(2)}) collective-permute-start(f32[16,60,128]{2,1,0:T(8,128)S(1)} %slice.405), channel_id=1, source_target_pairs={{32,0},{64,32},{96,64},{128,96},{160,128},{192,160},{224,192},{256... | collective-permute-start | bytes 1474568 | tf_op jit(solution)/shard_map/ppermute | solution.py:30
  471.0 52.5 %collective-permute-start.28 = (f32[16,60,128]{2,1,0:T(8,128)S(1)}, f32[16,60,128]{2,1,0:T(8,128)S(1)}, u32[]{:S(2)}, u32[]{:S(2)}) collective-permute-start(f32[16,60,128]{2,1,0:T(8,128)S(1)} %slice.405), channel_id=1, source_target_pairs={{0,32},{32,64},{64,96},{96,128},{128,160},{160,192},{192,224},{224... | collective-permute-start | bytes 1474568 | tf_op jit(solution)/shard_map/ppermute | solution.py:30
  523.9 59.1 %collective-permute-start.30 = (f32[16,6,384]{2,1,0:T(8,128)S(1)}, f32[16,6,384]{2,1,0:T(8,128)S(1)}, u32[]{:S(2)}, u32[]{:S(2)}) collective-permute-start(f32[16,6,384]{2,1,0:T(8,128)S(1)} %get-tuple-element.194), channel_id=1, source_target_pairs={{0,1},{1,2},{2,3},{3,4},{4,5},{5,6},{6,7},{7,8},{8,9},{9,10},{10,1... | collective-permute-start | bytes 442376 | tf_op jit(solution)/shard_map/ppermute | solution.py:30
  525.8 57.2 %collective-permute-start.31 = (f32[16,6,384]{2,1,0:T(8,128)S(1)}, f32[16,6,384]{2,1,0:T(8,128)S(1)}, u32[]{:S(2)}, u32[]{:S(2)}) collective-permute-start(f32[16,6,384]{2,1,0:T(8,128)S(1)} %get-tuple-element.195), channel_id=1, source_target_pairs={{1,0},{2,1},{3,2},{4,3},{5,4},{6,5},{7,6},{8,7},{9,8},{10,9},{11,1... | collective-permute-start | bytes 442376 | tf_op jit(solution)/shard_map/ppermute | solution.py:30
  528.8 54.3 %copy-start.3 = (f32[16,48,384]{2,1,0:T(8,128)S(1)}, f32[16,48,384]{2,1,0:T(8,128)}, u32[]{:S(2)}) copy-start(f32[16,48,384]{2,1,0:T(8,128)} %get-tuple-element.233) | copy-start | bytes 3538948
  528.8 54.3 %copy-start.13 = (pred[48,384]{1,0:T(8,128)(4,1)S(1)}, pred[48,384]{1,0:T(8,128)(4,1)}, u32[]{:S(2)}) copy-start(pred[48,384]{1,0:T(8,128)(4,1)} %broadcast_or_fusion) | copy-start | bytes 55300
  528.8 54.3 %copy-start.21 = (f32[16]{0:T(128)S(1)}, f32[16]{0:T(128)}, u32[]{:S(2)}) copy-start(f32[16]{0:T(128)} %get-tuple-element.224) | copy-start | bytes 196
  528.8 54.3 %copy-start.23 = (f32[16]{0:T(128)S(1)}, f32[16]{0:T(128)}, u32[]{:S(2)}) copy-start(f32[16]{0:T(128)} %get-tuple-element.225) | copy-start | bytes 196
  528.8 54.3 %copy-start.32 = (f32[16]{0:T(128)S(1)}, f32[16]{0:T(128)}, u32[]{:S(2)}) copy-start(f32[16]{0:T(128)} %param.9) | copy-start | bytes 196
  528.8 33.7 %collective-permute-start.24 = (f32[16,48,1]{2,1,0:T(8,128)S(1)}, f32[16,48,1]{2,1,0:T(8,128)S(1)}, u32[]{:S(2)}, u32[]{:S(2)}) collective-permute-start(f32[16,48,1]{2,1,0:T(8,128)S(1)} %get-tuple-element.201), channel_id=1, source_target_pairs={{32,0},{64,32},{96,64},{128,96},{160,128},{192,160},{224,192},{256... | collective-permute-start | bytes 9224 | tf_op jit(solution)/shard_map/ppermute | solution.py:22
  530.9 40.4 %collective-permute-start.25 = (f32[16,48,1]{2,1,0:T(8,128)S(1)}, f32[16,48,1]{2,1,0:T(8,128)S(1)}, u32[]{:S(2)}, u32[]{:S(2)}) collective-permute-start(f32[16,48,1]{2,1,0:T(8,128)S(1)} %get-tuple-element.200), channel_id=1, source_target_pairs={{0,32},{32,64},{64,96},{96,128},{128,160},{160,192},{192,224},{224... | collective-permute-start | bytes 9224 | tf_op jit(solution)/shard_map/ppermute | solution.py:21
  571.6 10.7 %collective-permute-start.26 = (f32[16,1,386]{2,1,0:T(1,128)S(1)}, f32[16,1,386]{2,1,0:T(1,128)S(1)}, u32[]{:S(2)}, u32[]{:S(2)}) collective-permute-start(f32[16,1,386]{2,1,0:T(1,128)S(1)} %get-tuple-element.189), channel_id=1, source_target_pairs={{1,0},{2,1},{3,2},{4,3},{5,4},{6,5},{7,6},{8,7},{9,8},{10,9},{11,1... | collective-permute-start | bytes 74120 | tf_op jit(solution)/shard_map/ppermute | solution.py:22
  574.2 8.8 %collective-permute-start.27 = (f32[16,1,386]{2,1,0:T(1,128)S(1)}, f32[16,1,386]{2,1,0:T(1,128)S(1)}, u32[]{:S(2)}, u32[]{:S(2)}) collective-permute-start(f32[16,1,386]{2,1,0:T(1,128)S(1)} %get-tuple-element.188), channel_id=1, source_target_pairs={{0,1},{1,2},{2,3},{3,4},{4,5},{5,6},{6,7},{7,8},{8,9},{9,10},{10,1... | collective-permute-start | bytes 74120 | tf_op jit(solution)/shard_map/ppermute | solution.py:21
  619.4 14.0 %collective-permute-start.32 = (f32[16,16,1]{2,1,0:T(8,128)S(1)}, f32[16,16,1]{2,1,0:T(8,128)S(1)}, u32[]{:S(2)}, u32[]{:S(2)}) collective-permute-start(f32[16,16,1]{2,1,0:T(8,128)S(1)} %get-tuple-element.212), channel_id=1, source_target_pairs={{0,32},{32,64},{64,96},{96,128},{128,160},{160,192},{192,224},{224... | collective-permute-start | bytes 3080 | tf_op jit(solution)/shard_map/ppermute | solution.py:21
  621.6 15.1 %collective-permute-start.33 = (f32[16,16,1]{2,1,0:T(8,128)S(1)}, f32[16,16,1]{2,1,0:T(8,128)S(1)}, u32[]{:S(2)}, u32[]{:S(2)}) collective-permute-start(f32[16,16,1]{2,1,0:T(8,128)S(1)} %get-tuple-element.213), channel_id=1, source_target_pairs={{32,0},{64,32},{96,64},{128,96},{160,128},{192,160},{224,192},{256... | collective-permute-start | bytes 3080 | tf_op jit(solution)/shard_map/ppermute | solution.py:22
  636.9 9.6 %collective-permute-start.34 = (f32[16,1,130]{2,1,0:T(1,128)S(1)}, f32[16,1,130]{2,1,0:T(1,128)S(1)}, u32[]{:S(2)}, u32[]{:S(2)}) collective-permute-start(f32[16,1,130]{2,1,0:T(1,128)S(1)} %get-tuple-element.206), channel_id=1, source_target_pairs={{0,1},{1,2},{2,3},{3,4},{4,5},{5,6},{6,7},{7,8},{8,9},{9,10},{10,1... | collective-permute-start | bytes 24968 | tf_op jit(solution)/shard_map/ppermute | solution.py:21
  644.5 7.8 %collective-permute-start.35 = (f32[16,1,130]{2,1,0:T(1,128)S(1)}, f32[16,1,130]{2,1,0:T(1,128)S(1)}, u32[]{:S(2)}, u32[]{:S(2)}) collective-permute-start(f32[16,1,130]{2,1,0:T(1,128)S(1)} %get-tuple-element.207), channel_id=1, source_target_pairs={{1,0},{2,1},{3,2},{4,3},{5,4},{6,5},{7,6},{8,7},{9,8},{10,9},{11,1... | collective-permute-start | bytes 24968 | tf_op jit(solution)/shard_map/ppermute | solution.py:22
  (38 other events, 623.2 us)
where the time goes:
time: 658 us; the launch traced here: 653 us
  waiting for transfers between devices  220 us (33%)
  local copies, waits for them, and re-layouts  209 us (32%)
  starting transfers between devices  175 us (27%)
  other arithmetic  32.7 us (5%)
  matrix products  14.3 us (2%)
    gather x192, local copies, waits for them, and re-layouts  158 us
    ppermute x12, waiting for transfers between devices, shifted(): return lax.ppermute(block, axis, route)  95.8 us
    ppermute x12, starting transfers between devices, extended_2(): before = lax.ppermute(last, axis, up)  78.8 us
    ppermute x12, waiting for transfers between devices, extended_2(): before = lax.ppermute(last, axis, up)  68.6 us
    ppermute x12, waiting for transfers between devices, extended_2(): after = lax.ppermute(leading, axis, down)  55.7 us
    ppermute x12, starting transfers between devices, shifted(): return lax.ppermute(block, axis, route)  51.4 us
    ppermute x12, starting transfers between devices, extended_2(): after = lax.ppermute(leading, axis, down)  45.3 us
    unnamed x109, local copies, waits for them, and re-layouts  20.9 us
  transfers between devices with their start and end apart: 36, of which 19 were waited for; matrix products, arithmetic and copies ran while one was open for 3% of the time, Pallas kernels for 0%

commit v1 on v0

v1 whole, which is shorter than its diff:
```python
import functools

import jax
import jax.numpy as jnp
from jax import lax
from jax.experimental import pallas as pl
from jax.experimental.pallas import tpu as pltpu
from jax.sharding import PartitionSpec as P

C = 16
NYD = 48
NXD = 384
PYD = 16
PXD = 128
MAXD = 8
FOOT = 6
H = 16
PH = 8
ROWS = NYD + 2 * H
PROWS = PYD + 2 * PH
WIDE = 512
PWIDE = 256
SLOT = 80
CHUNK = 6
F32 = jnp.float32
BF16 = jnp.bfloat16
MESH = pl.DeviceIdType.MESH
AROUND = ((0, 0), (0, -1), (0, 1), (-1, 0), (1, 0), (-1, -1), (1, -1), (-1, 1), (1, 1))


def lanes_of(shape):
    return lax.broadcasted_iota(jnp.int32, shape, len(shape) - 1)


def turn(value, shift):
    shift = shift % value.shape[-1] if isinstance(shift, int) else shift
    if isinstance(shift, int) and shift == 0:
        return value
    return pltpu.roll(value, shift, value.ndim - 1)


def thrusts(wind, scale):
    half = C // 2
    east, north = wind[:half], wind[half:]
    speed = jnp.sqrt(east * east + north * north + 1.0)
    return scale * wind * jnp.concatenate([speed, speed], axis=0)


def exchange(tiles_x, tiles_y, nest, parent, sites, live, coef,
             own, south, north, pown, psouth, pnorth, west, east, corner, info,
             pack_w, pack_e, in_sem, send_sem, recv_sem):
    gx, gy = lax.axis_index("gx"), lax.axis_index("gy")

    def device(dx, dy):
        return (lax.rem(gx + dx + tiles_x, tiles_x), lax.rem(gy + dy + tiles_y, tiles_y))

    barrier = pltpu.get_barrier_semaphore()
    for dx, dy in AROUND[1:]:
        pl.semaphore_signal(barrier, inc=1, device_id=device(dx, dy), device_id_type=MESH)

    loads = [pltpu.make_async_copy(nest.at[c], own.at[:, c, :], in_sem.at[c]) for c in range(C)]
    loads += [pltpu.make_async_copy(parent.at[c], pown.at[:, c, :], in_sem.at[C + c]) for c in range(C)]
    for load in loads:
        load.start()
    for load in loads:
        load.wait()

    lane = lanes_of((C, PXD))
    wide_lane = lanes_of((C, NXD))
    wind = jnp.zeros((C, PXD), F32)
    scale = jnp.zeros((C, PXD), F32)
    spot = jnp.zeros((C, PXD), F32)
    for s in range(MAXD):
        row, col = sites[0, 0, 0, s], sites[1, 0, 0, s]
        line = own[row]
        value = jnp.sum(jnp.where(wide_lane == col, line, 0.0), axis=1, keepdims=True)
        wind = jnp.where(lane == s, value, wind)
        push = -(coef[0, 0, s] * live[0, 0, s].astype(F32))
        scale = jnp.where(lane == s, push, scale)
        spot = jnp.where(lane == MAXD + s, row.astype(F32), spot)
        spot = jnp.where(lane == 2 * MAXD + s, col.astype(F32), spot)
        spot = jnp.where(lane == 3 * MAXD + s, push, spot)
    mine = thrusts(wind, scale) + spot
    info[0] = mine

    for pack, tile, first in ((pack_w, 0, 0), (pack_e, NXD // 128 - 1, 112)):
        for p in range(NYD // 8):
            packed = jnp.zeros((C, 128), F32)
            for j in range(8):
                cells = own[8 * p + j, :, 128 * tile : 128 * tile + 128]
                packed = jnp.where(lane // 16 == j, turn(cells, 16 * j - first), packed)
            pack[2 + p] = packed
    for pack, first in ((pack_w, 0), (pack_e, 120)):
        packed = jnp.zeros((C, 128), F32)
        for m in range(PYD):
            packed = jnp.where(lane // 8 == m, turn(pown[m], 8 * m - first), packed)
        pack[0] = packed
        pack[1] = mine
        pack[8] = packed
        pack[9] = mine

    sends = (
        (pack_e.at[pl.ds(6, 4)], corner.at[0], (1, 1)),
        (pack_w.at[pl.ds(6, 4)], corner.at[1], (-1, 1)),
        (pack_e.at[pl.ds(0, 4)], corner.at[2], (1, -1)),
        (pack_w.at[pl.ds(0, 4)], corner.at[3], (-1, -1)),
        (pack_e.at[pl.ds(0, 8)], west, (1, 0)),
        (pack_w.at[pl.ds(0, 8)], east, (-1, 0)),
        (own.at[pl.ds(NYD - H, H)], south, (0, 1)),
        (own.at[pl.ds(0, H)], north, (0, -1)),
        (pown.at[pl.ds(PYD - PH, PH)], psouth, (0, 1)),
        (pown.at[pl.ds(0, PH)], pnorth, (0, -1)),
        (info.at[0], info.at[1], (0, 1)),
        (info.at[0], info.at[2], (0, -1)),
    )
    pl.semaphore_wait(barrier, len(AROUND) - 1)
    copies = []
    for i, (source, target, (dx, dy)) in enumerate(sends):
        copy = pltpu.make_async_remote_copy(
            src_ref=source, dst_ref=target, send_sem=send_sem.at[i], recv_sem=recv_sem.at[i],
            device_id=device(dx, dy), device_id_type=MESH,
        )
        copy.start()
        copies.append(copy)
    for copy in copies:
        copy.wait()


def advance_all(tiles_x, tiles_y, diffusion, drift, own, south, north, pown, psouth, pnorth, west, east, corner, info,
                nest_out, parent_out,
                one, two, old, new, cols_old, cols_new, lines, row_g, col_g, places, out_v, sum_v, place_sem, out_sem):
    gx, gy = lax.axis_index("gx"), lax.axis_index("gy")
    lane = lanes_of((C, 128))
    notes = (info.at[0], info.at[1], info.at[2], west.at[1], east.at[1],
             corner.at[0, 3], corner.at[1, 3], corner.at[2, 1], corner.at[3, 1])
    moves = [pltpu.make_async_copy(note.at[pl.ds(0, 8)], places.at[j], place_sem.at[j]) for j, note in enumerate(notes)]
    for move in moves:
        move.start()

    has_w, has_e = (gx > 0).astype(F32), (gx < tiles_x - 1).astype(F32)
    has_s, has_n = (gy > 0).astype(F32), (gy < tiles_y - 1).astype(F32)
    of_x = {-1: has_w, 0: None, 1: has_e}
    of_y = {-1: has_s, 0: None, 1: has_n}

    push = jnp.zeros((C, 128), F32)
    scale = jnp.zeros((C, 128), F32)
    disk_rows = jnp.full((C, 128), 1.0e6, F32)
    disk_cols = jnp.full((C, 128), 1.0e6, F32)
    for j, (dx, dy) in enumerate(AROUND):
        note = notes[j][...]
        here = lane // MAXD == j
        first, force = turn(note, MAXD * j), turn(note, MAXD * j - 3 * MAXD)
        for there in (of_x[dx], of_y[dy]):
            if there is not None:
                first, force = first * there, force * there
        push = jnp.where(here, first, push)
        scale = jnp.where(here, force, scale)
        disk_rows = jnp.where(here, turn(note, MAXD * j - MAXD) + float(H + NYD * dy), disk_rows)
        disk_cols = jnp.where(here, turn(note, MAXD * j - 2 * MAXD) + float(NXD * dx), disk_cols)

    def thrice(value):
        shape = value.shape
        at = lanes_of(shape)
        later = turn(value, SLOT)
        return (jnp.where(at < SLOT, value, later),
                jnp.where(at < 2 * SLOT - 128, later, turn(value, 2 * SLOT - 128)))

    def profile(distance):
        return jnp.where(jnp.abs(distance) <= float(FOOT), jnp.exp(distance * distance * (-1.0 / 8.0)), 0.0)

    rows_2 = thrice(disk_rows[0:8])
    height = lax.broadcasted_iota(jnp.int32, (8, 128), 0).astype(F32)
    for block in range(ROWS // 8):
        for half in range(2):
            value = profile(height + float(8 * block) - rows_2[half])
            for j in range(8):
                row_g[8 * block + j, :, 128 * half : 128 * half + 128] = value[j : j + 1]
    cols_2 = thrice(disk_cols[0:8])
    depth_at = lax.broadcasted_iota(jnp.int32, (128, 128), 0)
    for half in range(2):
        across = jnp.transpose(jnp.broadcast_to(cols_2[half][0:1], (128, 128)))
        third = depth_at + 128 * half >= 2 * SLOT
        for tile in range(WIDE // 128):
            at = lanes_of((128, 128)) + 128 * tile
            at = jnp.where(at < 448, at, at - WIDE).astype(F32)
            value = profile(at - across)
            rest = value - value.astype(BF16).astype(F32)
            col_g[128 * half : 128 * half + 128, 128 * tile : 128 * tile + 128] = jnp.where(third, rest, value).astype(BF16)

    def copy_rows(source, base, count):
        def body(i, carry):
            one[base + i, :, 0:NXD] = source[i]
            return carry
        lax.fori_loop(0, count, body, 0)

    copy_rows(south, 0, H)
    copy_rows(own, H, NYD)
    copy_rows(north, H + NYD, H)
    for p in range(ROWS // 8):
        if p < 2:
            from_w, from_e = corner[0, p], corner[1, p]
        elif p < 8:
            from_w, from_e = west[p], east[p]
        else:
            from_w, from_e = corner[2, p - 6], corner[3, p - 6]
        for j in range(8):
            one[8 * p + j, :, NXD:WIDE] = jnp.where(
                lane < 16, turn(from_e, -16 * j), jnp.where(lane >= 112, turn(from_w, 112 - 16 * j), 0.0))

    plane = lax.broadcasted_iota(jnp.int32, (C, 128), 0)

    def per_plane(read):
        value = jnp.zeros((C, 128), F32)
        for c in range(C):
            value = jnp.where(plane == c, read(c), value)
        return value

    spread = per_plane(lambda c: diffusion[c])
    east_by = per_plane(lambda c: drift[0, c])
    north_by = per_plane(lambda c: drift[1, c])

    def stencil(a):
        return (1.0 - 4.0 * a - east_by - north_by, a + east_by, a, a + north_by, a)

    def shifted(tiles):
        count = len(tiles)
        up = [turn(v, 1) for v in tiles]
        down = [turn(v, -1) for v in tiles]
        from_w = [jnp.where(lane == 0, up[(t - 1) % count], up[t]) for t in range(count)]
        from_e = [jnp.where(lane == 127, down[(t + 1) % count], down[t]) for t in range(count)]
        return from_w, from_e

    for block, (source, there, strips) in enumerate((
        (psouth, has_s, (corner[0, 2], corner[1, 2], 8)),
        (pown, None, (west[0], east[0], 0)),
        (pnorth, has_n, (corner[2, 0], corner[3, 0], 0)),
    )):
        base = (0, PH, PH + PYD)[block]
        count = (PH, PYD, PH)[block]
        for i in range(count):
            middle = source[i]
            m = i + strips[2]
            side = jnp.where(lane < 8, turn(strips[1], -8 * m) * has_e,
                             jnp.where(lane >= 120, turn(strips[0], 120 - 8 * m) * has_w, 0.0))
            if there is not None:
                middle, side = middle * there, side * there
            old[base + i, :, 0:128] = middle
            old[base + i, :, 128:256] = side
    kept = jnp.where(lane < 64, has_e, has_w)
    stay, cw, ce, cs, cn = stencil(spread * (1.0 / 3.0))
    new[0] = jnp.zeros((C, PWIDE), F32)
    new[PROWS - 1] = jnp.zeros((C, PWIDE), F32)

    def parent_row(i, carry):
        inside = jnp.where(i < PH, has_s, jnp.where(i >= PH + PYD, has_n, 1.0))
        tiles = [old[i, :, 128 * t : 128 * t + 128] for t in range(2)]
        from_w, from_e = shifted(tiles)
        for t in range(2):
            value = (stay * tiles[t] + cw * from_w[t] + ce * from_e[t]
                     + cs * old[i - 1, :, 128 * t : 128 * t + 128] + cn * old[i + 1, :, 128 * t : 128 * t + 128])
            value = value * inside
            new[i, :, 128 * t : 128 * t + 128] = value * kept if t == 1 else value
        return carry

    lax.fori_loop(1, PROWS - 1, parent_row, 0)

    @pl.when((gx == 0) | (gx == tiles_x - 1))
    def _():
        for source, target in ((old, cols_old), (new, cols_new)):
            for y in range(ROWS):
                q, rest = (y - H) // 3 + PH, (y - H) % 3
                centre = source[q, :, 0:128]
                if rest == 1:
                    value = centre * (2.0 / 3.0)
                else:
                    value = centre * (4.0 / 9.0) + source[q - 1 if rest == 0 else q + 1, :, 0:128] * (2.0 / 9.0)
                target[y] = value

    def pieces(value, count):
        out = []
        for _ in range(count):
            part = value.astype(BF16)
            out.append(part)
            value = value - part.astype(F32)
        return out

    @pl.when((gy == 0) | (gy == tiles_y - 1))
    def _():
        fine = lanes_of((PWIDE, WIDE))
        fine = jnp.where(fine < 448, fine, fine - WIDE)
        coarse = lax.broadcasted_iota(jnp.int32, (PWIDE, WIDE), 0)
        coarse = jnp.where(coarse < 192, coarse, coarse - PWIDE)
        hat = jnp.maximum(3 - jnp.abs(fine - (3 * coarse + 1)), 0).astype(F32).astype(BF16)
        at = jnp.where(gy == 0, PH, PH + PYD - 1)
        parts = pieces(old[at], 3) + pieces(new[at], 3)
        for i in range(2):
            total = jnp.zeros((C, WIDE), F32)
            for part in parts[3 * i : 3 * i + 3]:
                total = total + jnp.dot(part, hat, preferred_element_type=F32)
            lines[i] = total * (2.0 / 9.0)

    stay, cw, ce, cs, cn = stencil(spread)
    second = [lane + 128 * half for half in range(2)]
    second = [(at >= SLOT) & (at < 2 * SLOT) for at in second]

    def step(source, target, amounts, low, high, k):
        amounts_2 = thrice(amounts)

        def body(i, carry):
            base = low + CHUNK * i
            left = []
            for r in range(CHUNK):
                halves = []
                for half in range(2):
                    value = amounts_2[half] * row_g[base + r, :, 128 * half : 128 * half + 128]
                    rest = value - value.astype(BF16).astype(F32)
                    halves.append(jnp.where(second[half], rest, value).astype(BF16))
                left.append(jnp.concatenate(halves, axis=1))
            force = jnp.dot(jnp.concatenate(left, axis=0), col_g[...], preferred_element_type=F32)
            for r in range(CHUNK):
                y = base + r
                tiles = [source[y, :, 128 * t : 128 * t + 128] for t in range(4)]
                from_w, from_e = shifted(tiles)
                for t in range(4):
                    at = slice(128 * t, 128 * t + 128)
                    target[y, :, at] = (
                        stay * tiles[t] + cw * from_w[t] + ce * from_e[t] + cs * source[y - 1, :, at]
                        + cn * source[y + 1, :, at] + force[C * r : C * r + C, at])
            return carry

        lax.fori_loop(0, (high - low) // CHUNK, body, 0)

        for edge, tile, spot in ((0, 0, 0), (tiles_x - 1, NXD // 128 - 1, 127)):
            @pl.when(gx == edge)
            def _():
                def patch(i, carry):
                    at = slice(128 * tile, 128 * tile + 128)
                    bound = cols_old[i] + (k / 3.0) * (cols_new[i] - cols_old[i])
                    target[i, :, at] = jnp.where(lane == spot, bound, target[i, :, at])
                    return carry
                lax.fori_loop(low, high, patch, 0)
        for edge, row in ((0, H), (tiles_y - 1, H + NYD - 1)):
            @pl.when(gy == edge)
            def _():
                target[row] = lines[0] + (k / 3.0) * (lines[1] - lines[0])

    def gathered(source):
        wind = jnp.zeros((C, 128), F32)
        for j, (dx, dy) in enumerate(AROUND):
            for s in range(MAXD):
                d = MAXD * j + s
                row = places[j, 0, MAXD + s].astype(jnp.int32) + (H + NYD * dy)
                col = places[j, 0, 2 * MAXD + s].astype(jnp.int32) + NXD * dx
                row = jnp.clip(row, 0, ROWS - 1)
                col = jnp.bitwise_and(col, WIDE - 1)
                tile = pl.multiple_of(jnp.bitwise_and(col, WIDE - 128), 128)
                cells = source[row, :, pl.ds(tile, 128)]
                wind = jnp.where(lane == d, turn(cells, jnp.bitwise_and(d - col, 127)), wind)
        return wind

    for buffer, rows in ((two, (0, ROWS - 1)),):
        for row in rows:
            buffer[row] = jnp.zeros((C, WIDE), F32)

    step(one, two, push, 1, ROWS - 1, 1)
    for move in moves:
        move.wait()
    push = thrusts(gathered(two), scale)
    step(two, one, push, 7, ROWS - 7, 2)
    push = thrusts(gathered(one), scale)
    step(one, two, push, 13, ROWS - 13, 3)

    stores = [pltpu.make_async_copy(two.at[pl.ds(H, NYD), c, pl.ds(0, NXD)], nest_out.at[c], out_sem.at[c]) for c in range(C)]
    for store in stores:
        store.start()

    low_side = jnp.where(gx == 0, 0, -64)
    high_side = jnp.where(gx == tiles_x - 1, NXD, NXD + 64)
    fine = lax.broadcasted_iota(jnp.int32, (WIDE, 128), 0)
    fine = jnp.where(fine < 448, fine, fine - WIDE)
    gap = jnp.abs(fine - (3 * lanes_of((WIDE, 128)) + 1))
    weight = jnp.where(gap <= 1, 2.0, jnp.where(gap <= 4, 1.0, 0.0))
    weight = jnp.where((fine >= low_side) & (fine < high_side), weight, 0.0).astype(BF16)

    def three(m):
        y = H + 3 * m
        return two[y] + two[y + 1] + two[y + 2]

    before, here = three(-1) * has_s, three(0)
    high_part, low_part = [], []
    for m in range(PYD):
        after = three(m + 1)
        if m == PYD - 1:
            after = after * has_n
        total = before + 2.0 * here + after
        part = pieces(total, 2)
        sum_v[C * m : C * m + C] = part[0]
        sum_v[C * (PYD + m) : C * (PYD + m) + C] = part[1]
        before, here = here, after
    mean = jnp.dot(sum_v[...], weight, preferred_element_type=F32)
    half = C * PYD
    for m in range(PYD):
        i = m + PH
        tiles = [new[i - 1, :, 128 * t : 128 * t + 128] + 2.0 * new[i, :, 128 * t : 128 * t + 128]
                 + new[i + 1, :, 128 * t : 128 * t + 128] for t in range(2)]
        from_w, from_e = shifted(tiles)
        direct = from_w[0] + 2.0 * tiles[0] + from_e[0]
        out_v[m] = direct * (1.0 / 32.0) + (mean[C * m : C * m + C] + mean[half + C * m : half + C * m + C]) * (1.0 / 288.0)
    last = [pltpu.make_async_copy(out_v.at[:, c, :], parent_out.at[c], out_sem.at[C + c]) for c in range(C)]
    for store in last:
        store.start()
    for store in stores + last:
        store.wait()


def solution(mesh):
    tiles_x, tiles_y = mesh.shape["gx"], mesh.shape["gy"]
    smem = pl.BlockSpec(memory_space=pltpu.SMEM)
    vmem = pl.BlockSpec(memory_space=pltpu.VMEM)
    anywhere = pl.BlockSpec(memory_space=pl.ANY)
    passed = ((NYD, C, NXD), (H, C, NXD), (H, C, NXD), (PYD, C, PXD), (PH, C, PXD), (PH, C, PXD),
              (8, C, 128), (8, C, 128), (4, 4, C, 128), (3, C, 128))

    def on_device(nest_wind, parent_wind, diffusion, drift, disk_sites, disk_live, disk_coef):
        rims = pl.pallas_call(
            functools.partial(exchange, tiles_x, tiles_y),
            out_shape=[pltpu.VMEM(shape, F32) for shape in passed],
            in_specs=[anywhere, anywhere, smem, smem, smem],
            out_specs=[vmem] * len(passed),
            scratch_shapes=[
                pltpu.VMEM((10, C, 128), F32),
                pltpu.VMEM((10, C, 128), F32),
                pltpu.SemaphoreType.DMA((2 * C,)),
                pltpu.SemaphoreType.DMA((12,)),
                pltpu.SemaphoreType.DMA((12,)),
            ],
            compiler_params=pltpu.CompilerParams(
                collective_id=0, has_side_effects=True, vmem_limit_bytes=16 * 2**20),
            name="exchange",
        )(nest_wind, parent_wind, disk_sites, disk_live, disk_coef)
        return tuple(pl.pallas_call(
            functools.partial(advance_all, tiles_x, tiles_y),
            out_shape=[jax.ShapeDtypeStruct(nest_wind.shape, F32), jax.ShapeDtypeStruct(parent_wind.shape, F32)],
            in_specs=[smem, smem] + [vmem] * len(passed),
            out_specs=[anywhere, anywhere],
            scratch_shapes=[
                pltpu.VMEM((ROWS, C, WIDE), F32),
                pltpu.VMEM((ROWS, C, WIDE), F32),
                pltpu.VMEM((PROWS, C, PWIDE), F32),
                pltpu.VMEM((PROWS, C, PWIDE), F32),
                pltpu.VMEM((ROWS, C, 128), F32),
                pltpu.VMEM((ROWS, C, 128), F32),
                pltpu.VMEM((2, C, WIDE), F32),
                pltpu.VMEM((ROWS, 1, 256), F32),
                pltpu.VMEM((256, WIDE), BF16),
                pltpu.SMEM((9, 8, 128), F32),
                pltpu.VMEM((PYD, C, PXD), F32),
                pltpu.VMEM((2 * C * PYD, WIDE), BF16),
                pltpu.SemaphoreType.DMA((9,)),
                pltpu.SemaphoreType.DMA((2 * C,)),
            ],
            compiler_params=pltpu.CompilerParams(vmem_limit_bytes=40 * 2**20),
            name="advance",
        )(diffusion, drift, *rims))

    placed = (
        P(None, "gy", "gx"),
        P(None, "gy", "gx"),
        P(),
        P(),
        P(None, "gy", "gx", None),
        P("gy", "gx", None),
        P("gy", "gx", None),
    )
    return jax.shard_map(
        on_device,
        mesh=mesh,
        in_specs=placed,
        out_specs=(P(None, "gy", "gx"), P(None, "gy", "gx")),
        check_vma=False,
    )
```

time: 658 us -> 59.6 us (0.09)
  the two profiles are of different devices: /device:TPU:109 before, /device:TPU:24 now
where the time goes in v1:
time: 59.6 us; the launch traced here: 59.2 us
  Pallas kernels  54.3 us (91%)
  local copies, waits for them, and re-layouts  4.16 us (7%)
  between operations  0.67 us (1%)
    pallas_call x1, Pallas kernels, on_device(): pl.pallas_call(functools.partial(exchange, tiles_x, tiles_y), out_shape=[...  39.2 us
    pallas_call x1, Pallas kernels, on_device(): pl.pallas_call(functools.partial(advance_all, tiles_x, tiles_y), out_shap...  15.2 us
    unnamed x14, local copies, waits for them, and re-layouts  4.16 us

profile of v1, /device:TPU:24, one launch (start us, length us, event | category | flops | bytes accessed | tf_op | source)
XLA Modules:
  0.0 59.2 jit_solution(1527651353730969623)
XLA Ops:
  0.6 0.0 copy-start
  0.6 1.3 %copy-done = f32[16,48,384]{2,1,0:T(8,128)S(1)} copy-done((f32[16,48,384]{2,1,0:T(8,128)S(1)}, f32[16,48,384]{2,1,0:T(8,128)}, u32[]{:S(2)}) %copy-start) | copy-done | bytes 1179672
  1.9 0.0 copy-start.1
  1.9 0.9 %copy-done.1 = f32[16,16,128]{2,1,0:T(8,128)S(1)} copy-done((f32[16,16,128]{2,1,0:T(8,128)S(1)}, f32[16,16,128]{2,1,0:T(8,128)}, u32[]{:S(2)}) %copy-start.1) | copy-done | bytes 131096
  2.8 0.0 copy-start.3
  2.8 0.7 %copy-done.3 = s32[2,1,1,8]{3,2,1,0:T(1,128)S(1)} copy-done((s32[2,1,1,8]{3,2,1,0:T(1,128)S(1)}, s32[2,1,1,8]{3,2,1,0:T(1,128)}, u32[]{:S(2)}) %copy-start.3) | copy-done | bytes 88
  3.5 0.0 copy-start.4
  3.5 0.7 %copy-done.4 = s32[1,1,8]{2,1,0:T(1,128)S(1)} copy-done((s32[1,1,8]{2,1,0:T(1,128)S(1)}, s32[1,1,8]{2,1,0:T(1,128)}, u32[]{:S(2)}) %copy-start.4) | copy-done | bytes 56
  4.1 0.0 copy-start.5
  4.1 0.7 %copy-done.5 = f32[1,1,8]{2,1,0:T(1,128)S(1)} copy-done((f32[1,1,8]{2,1,0:T(1,128)S(1)}, f32[1,1,8]{2,1,0:T(1,128)}, u32[]{:S(2)}) %copy-start.5) | copy-done | bytes 56
  4.8 0.0 copy-start.2
  4.8 0.0 copy-start.6
  4.8 39.2 %exchange.1 = (f32[48,16,384]{2,1,0:T(8,128)S(1)}, f32[16,16,384]{2,1,0:T(8,128)S(1)}, f32[16,16,384]{2,1,0:T(8,128)S(1)}, f32[16,16,128]{2,1,0:T(8,128)S(1)}, f...) custom-call(f32[16,48,384]{2,1,0:T(8,128)S(1)} %copy-done, ...), custom_call_target="tpu_custom_call" | custom-call | tf_op jit(solution)/shard_map/exchange/pallas_call | solution.py:425
  44.0 0.0 copy-done.2
  44.0 0.0 copy-done.6
  44.0 15.2 %advance.1 = (f32[16,48,384]{2,1,0:T(8,128)}, f32[16,16,128]{2,1,0:T(8,128)}) custom-call(f32[16]{0:T(128)S(1)} %copy-done.6, f32[2,16]{1,0:T(2,128)S(1)} %copy-done.2, f32[48,16,384]{2,1,0:T(8,128)S(1)} %get-tuple-element.12.own, f32[16,16,384]{2,1,0:T(8,128)S(1)} %get-tuple-element.13.south, f32[16,16,384]{2,1,0:T(8,128)S(1)} %get-tuple-element.14.north, ...), custom_call_target="tpu_custom_call" | custom-call | tf_op jit(solution)/shard_map/advance/pallas_call | solution.py:441
Async XLA Ops:
  0.6 1.3 %copy-start = (f32[16,48,384]{2,1,0:T(8,128)S(1)}, f32[16,48,384]{2,1,0:T(8,128)}, u32[]{:S(2)}) copy-start(f32[16,48,384]{2,1,0:T(8,128)} %nest.1) | copy-start | bytes 3538948
  1.9 0.9 %copy-start.1 = (f32[16,16,128]{2,1,0:T(8,128)S(1)}, f32[16,16,128]{2,1,0:T(8,128)}, u32[]{:S(2)}) copy-start(f32[16,16,128]{2,1,0:T(8,128)} %parent.1) | copy-start | bytes 393220
  2.8 0.7 %copy-start.3 = (s32[2,1,1,8]{3,2,1,0:T(1,128)S(1)}, s32[2,1,1,8]{3,2,1,0:T(1,128)}, u32[]{:S(2)}) copy-start(s32[2,1,1,8]{3,2,1,0:T(1,128)} %sites.1) | copy-start | bytes 196
  3.5 0.7 %copy-start.4 = (s32[1,1,8]{2,1,0:T(1,128)S(1)}, s32[1,1,8]{2,1,0:T(1,128)}, u32[]{:S(2)}) copy-start(s32[1,1,8]{2,1,0:T(1,128)} %live.1) | copy-start | bytes 100
  4.1 0.7 %copy-start.5 = (f32[1,1,8]{2,1,0:T(1,128)S(1)}, f32[1,1,8]{2,1,0:T(1,128)}, u32[]{:S(2)}) copy-start(f32[1,1,8]{2,1,0:T(1,128)} %coef.1) | copy-start | bytes 100
  4.8 39.2 %copy-start.2 = (f32[2,16]{1,0:T(2,128)S(1)}, f32[2,16]{1,0:T(2,128)}, u32[]{:S(2)}) copy-start(f32[2,16]{1,0:T(2,128)} %drift.1) | copy-start | bytes 388
  4.8 39.2 %copy-start.6 = (f32[16]{0:T(128)S(1)}, f32[16]{0:T(128)}, u32[]{:S(2)}) copy-start(f32[16]{0:T(128)} %diffusion.1) | copy-start | bytes 196

commit v2 on v1

--- a/solution.py
+++ b/solution.py
@@ -16,6 +16,8 @@
 FOOT = 6
 H = 16
 PH = 8
+NEAR = 6
+PNEAR = 2
 ROWS = NYD + 2 * H
 PROWS = PYD + 2 * PH
 WIDE = 512
@@ -46,9 +48,21 @@
     return scale * wind * jnp.concatenate([speed, speed], axis=0)
 
 
-def exchange(tiles_x, tiles_y, nest, parent, sites, live, coef,
-             own, south, north, pown, psouth, pnorth, west, east, corner, info,
-             pack_w, pack_e, in_sem, send_sem, recv_sem):
+def plane_tile(read):
+    at = lax.broadcasted_iota(jnp.int32, (C, 128), 0)
+    value = jnp.zeros((C, 128), F32)
+    for c in range(C):
+        value = jnp.where(at == c, read(c), value)
+    return value
+
+
+def factors(spread, east_by, north_by):
+    return (1.0 - 4.0 * spread - east_by - north_by, spread + east_by, spread, spread + north_by, spread)
+
+
+def exchange(tiles_x, tiles_y, nest, parent, diffusion_h, drift_h, sites_h, live_h, coef_h,
+             own, south, north, pown, psouth, pnorth, west, east, corner, info, sides,
+             pack_w, pack_e, diffusion, drift, sites, live, coef, in_sem, send_sem, recv_sem):
     gx, gy = lax.axis_index("gx"), lax.axis_index("gy")
 
     def device(dx, dy):
@@ -58,31 +72,16 @@
     for dx, dy in AROUND[1:]:
         pl.semaphore_signal(barrier, inc=1, device_id=device(dx, dy), device_id_type=MESH)
 
+    small = ((diffusion_h, diffusion), (drift_h, drift), (sites_h, sites), (live_h, live), (coef_h, coef))
     loads = [pltpu.make_async_copy(nest.at[c], own.at[:, c, :], in_sem.at[c]) for c in range(C)]
     loads += [pltpu.make_async_copy(parent.at[c], pown.at[:, c, :], in_sem.at[C + c]) for c in range(C)]
+    loads += [pltpu.make_async_copy(a, b, in_sem.at[2 * C + i]) for i, (a, b) in enumerate(small)]
     for load in loads:
         load.start()
     for load in loads:
         load.wait()
 
     lane = lanes_of((C, PXD))
-    wide_lane = lanes_of((C, NXD))
-    wind = jnp.zeros((C, PXD), F32)
-    scale = jnp.zeros((C, PXD), F32)
-    spot = jnp.zeros((C, PXD), F32)
-    for s in range(MAXD):
-        row, col = sites[0, 0, 0, s], sites[1, 0, 0, s]
-        line = own[row]
-        value = jnp.sum(jnp.where(wide_lane == col, line, 0.0), axis=1, keepdims=True)
-        wind = jnp.where(lane == s, value, wind)
-        push = -(coef[0, 0, s] * live[0, 0, s].astype(F32))
-        scale = jnp.where(lane == s, push, scale)
-        spot = jnp.where(lane == MAXD + s, row.astype(F32), spot)
-        spot = jnp.where(lane == 2 * MAXD + s, col.astype(F32), spot)
-        spot = jnp.where(lane == 3 * MAXD + s, push, spot)
-    mine = thrusts(wind, scale) + spot
-    info[0] = mine
-
     for pack, tile, first in ((pack_w, 0, 0), (pack_e, NXD // 128 - 1, 112)):
         for p in range(NYD // 8):
             packed = jnp.zeros((C, 128), F32)
@@ -95,9 +94,68 @@
         for m in range(PYD):
             packed = jnp.where(lane // 8 == m, turn(pown[m], 8 * m - first), packed)
         pack[0] = packed
+        pack[8] = packed
+
+    wide_lane = lanes_of((C, NXD))
+    inner = (wide_lane >= H) & (wide_lane < NXD - H)
+    stay, cw, ce, cs, cn = factors(
+        plane_tile(lambda c: diffusion[c]), plane_tile(lambda c: drift[0, c]), plane_tile(lambda c: drift[1, c]))
+    middle = stay * stay + 2.0 * (cw * ce + cs * cn)
+
+    def three(value):
+        return jnp.concatenate([value] * (NXD // 128), axis=1)
+
+    row_weights = [three(v) for v in (cw, stay, ce)]
+    square_weights = [three(v) for v in (cw * cw, 2.0 * cw * stay, middle, 2.0 * stay * ce, ce * ce)]
+    wind = jnp.zeros((C, PXD), F32)
+    scale = jnp.zeros((C, PXD), F32)
+    spot = jnp.zeros((C, PXD), F32)
+    rests = [jnp.zeros((C, PXD), F32)] * 2
+
+    def total(value):
+        return jnp.sum(value, axis=1, keepdims=True)
+
+    for s in range(MAXD):
+        row, col = sites[0, 0, 0, s], sites[1, 0, 0, s]
+        gap = wide_lane - col
+        at_0 = gap == 0
+        value = total(jnp.where(at_0, own[row], 0.0))
+        wind = jnp.where(lane == s, value, wind)
+        push = -(coef[0, 0, s] * live[0, 0, s].astype(F32))
+        scale = jnp.where(lane == s, push, scale)
+        spot = jnp.where(lane == MAXD + s, row.astype(F32), spot)
+        spot = jnp.where(lane == 2 * MAXD + s, col.astype(F32), spot)
+        spot = jnp.where(lane == 3 * MAXD + s, push, spot)
+        line = jnp.where(gap == -1, row_weights[0], jnp.where(at_0, row_weights[1], jnp.where(gap == 1, row_weights[2], 0.0)))
+        square = jnp.zeros((C, NXD), F32)
+        for j in range(5):
+            square = jnp.where(gap == j - 2, square_weights[j], square)
+        near = {r: jnp.where(inner, own[jnp.clip(row + r, 0, NYD - 1)], 0.0) for r in range(-2, 3)}
+        along = {r: total(line * near[r]) for r in range(-1, 2)}
+        point = {r: total(jnp.where(at_0, near[r], 0.0)) for r in (-2, -1, 1, 2)}
+        ones = {0: along[0], -1: cs * point[-1], 1: cn * point[1]}
+        twos = {0: total(square * near[0]), -1: 2.0 * cs * along[-1], 1: 2.0 * cn * along[1],
+                -2: cs * cs * point[-2], 2: cn * cn * point[2]}
+        for way, (low, high) in enumerate(((NEAR, NYD - 1), (0, NYD - 1 - NEAR))):
+            for terms, at in ((ones, 4 * MAXD + s), (twos, 5 * MAXD + s)):
+                value = jnp.zeros((C, 128), F32)
+                for r, term in terms.items():
+                    value = value + term * ((row + r >= low) & (row + r <= high)).astype(F32)
+                rests[way] = jnp.where(lane == at, value, rests[way])
+    mine = thrusts(wind, scale) + spot
+    info[0] = mine
+    for pack in (pack_w, pack_e):
         pack[1] = mine
-        pack[8] = packed
         pack[9] = mine
+    for way in range(2):
+        base = 10 + 7 * way
+        for i in range(2):
+            first = 2 + i if way == 0 else 6 + i
+            pack_w[base + i] = pack_w[first]
+            pack_w[base + 2 + i] = pack_e[first]
+        pack_w[base + 4] = pack_w[0]
+        pack_w[base + 5] = pack_e[0]
+        pack_w[base + 6] = mine + rests[way]
 
     sends = (
         (pack_e.at[pl.ds(6, 4)], corner.at[0], (1, 1)),
@@ -106,12 +164,12 @@
         (pack_w.at[pl.ds(0, 4)], corner.at[3], (-1, -1)),
         (pack_e.at[pl.ds(0, 8)], west, (1, 0)),
         (pack_w.at[pl.ds(0, 8)], east, (-1, 0)),
-        (own.at[pl.ds(NYD - H, H)], south, (0, 1)),
-        (own.at[pl.ds(0, H)], north, (0, -1)),
-        (pown.at[pl.ds(PYD - PH, PH)], psouth, (0, 1)),
-        (pown.at[pl.ds(0, PH)], pnorth, (0, -1)),
-        (info.at[0], info.at[1], (0, 1)),
-        (info.at[0], info.at[2], (0, -1)),
+        (own.at[pl.ds(NYD - NEAR, NEAR)], south, (0, 1)),
+        (own.at[pl.ds(0, NEAR)], north, (0, -1)),
+        (pown.at[pl.ds(PYD - PNEAR, PNEAR)], psouth, (0, 1)),
+        (pown.at[pl.ds(0, PNEAR)], pnorth, (0, -1)),
+        (pack_w.at[pl.ds(17, 7)], sides.at[0], (0, 1)),
+        (pack_w.at[pl.ds(10, 7)], sides.at[1], (0, -1)),
     )
     pl.semaphore_wait(barrier, len(AROUND) - 1)
     copies = []
@@ -126,12 +184,12 @@
         copy.wait()
 
 
-def advance_all(tiles_x, tiles_y, diffusion, drift, own, south, north, pown, psouth, pnorth, west, east, corner, info,
+def advance_all(tiles_x, tiles_y, diffusion, drift, own, south, north, pown, psouth, pnorth, west, east, corner, info, sides,
                 nest_out, parent_out,
                 one, two, old, new, cols_old, cols_new, lines, row_g, col_g, places, out_v, sum_v, place_sem, out_sem):
     gx, gy = lax.axis_index("gx"), lax.axis_index("gy")
     lane = lanes_of((C, 128))
-    notes = (info.at[0], info.at[1], info.at[2], west.at[1], east.at[1],
+    notes = (info.at[0], sides.at[0, 6], sides.at[1, 6], west.at[1], east.at[1],
              corner.at[0, 3], corner.at[1, 3], corner.at[2, 1], corner.at[3, 1])
     moves = [pltpu.make_async_copy(note.at[pl.ds(0, 8)], places.at[j], place_sem.at[j]) for j, note in enumerate(notes)]
     for move in moves:
@@ -146,6 +204,7 @@
     scale = jnp.zeros((C, 128), F32)
     disk_rows = jnp.full((C, 128), 1.0e6, F32)
     disk_cols = jnp.full((C, 128), 1.0e6, F32)
+    missing = [jnp.zeros((C, 128), F32)] * 2
     for j, (dx, dy) in enumerate(AROUND):
         note = notes[j][...]
         here = lane // MAXD == j
@@ -153,6 +212,8 @@
         for there in (of_x[dx], of_y[dy]):
             if there is not None:
                 first, force = first * there, force * there
+        if dx == 0 and dy != 0:
+            missing = [jnp.where(here, turn(note, MAXD * j - (4 + i) * MAXD), missing[i]) for i in range(2)]
         push = jnp.where(here, first, push)
         scale = jnp.where(here, force, scale)
         disk_rows = jnp.where(here, turn(note, MAXD * j - MAXD) + float(H + NYD * dy), disk_rows)
@@ -193,9 +254,9 @@
             return carry
         lax.fori_loop(0, count, body, 0)
 
-    copy_rows(south, 0, H)
+    copy_rows(south, H - NEAR, NEAR)
     copy_rows(own, H, NYD)
-    copy_rows(north, H + NYD, H)
+    copy_rows(north, H + NYD, NEAR)
     for p in range(ROWS // 8):
         if p < 2:
             from_w, from_e = corner[0, p], corner[1, p]
@@ -204,23 +265,18 @@
         else:
             from_w, from_e = corner[2, p - 6], corner[3, p - 6]
         for j in range(8):
-            one[8 * p + j, :, NXD:WIDE] = jnp.where(
+            y = 8 * p + j
+            one[y, :, NXD:WIDE] = jnp.where(
                 lane < 16, turn(from_e, -16 * j), jnp.where(lane >= 112, turn(from_w, 112 - 16 * j), 0.0))
-
-    plane = lax.broadcasted_iota(jnp.int32, (C, 128), 0)
-
-    def per_plane(read):
-        value = jnp.zeros((C, 128), F32)
-        for c in range(C):
-            value = jnp.where(plane == c, read(c), value)
-        return value
-
-    spread = per_plane(lambda c: diffusion[c])
-    east_by = per_plane(lambda c: drift[0, c])
-    north_by = per_plane(lambda c: drift[1, c])
-
-    def stencil(a):
-        return (1.0 - 4.0 * a - east_by - north_by, a + east_by, a, a + north_by, a)
+            if y < H - NEAR or y >= H + NYD + NEAR:
+                way, i = (0, p) if y < H else (1, p - 8)
+                one[y, :, 0:128] = jnp.where(lane < 16, turn(sides[way, i], -16 * j), 0.0)
+                one[y, :, 128 : NXD - 128] = jnp.zeros((C, NXD - 256), F32)
+                one[y, :, NXD - 128 : NXD] = jnp.where(lane >= 112, turn(sides[way, 2 + i], 112 - 16 * j), 0.0)
+
+    spread = plane_tile(lambda c: diffusion[c])
+    east_by = plane_tile(lambda c: drift[0, c])
+    north_by = plane_tile(lambda c: drift[1, c])
 
     def shifted(tiles):
         count = len(tiles)
@@ -238,8 +294,13 @@
         base = (0, PH, PH + PYD)[block]
         count = (PH, PYD, PH)[block]
         for i in range(count):
-            middle = source[i]
             m = i + strips[2]
+            if block == 0 and i < PH - PNEAR or block == 2 and i >= PNEAR:
+                way = block // 2
+                middle = jnp.where(lane < 8, turn(sides[way, 4], -8 * m),
+                                   jnp.where(lane >= 120, turn(sides[way, 5], 120 - 8 * m), 0.0))
+            else:
+                middle = source[i - (PH - PNEAR) if block == 0 else i]
             side = jnp.where(lane < 8, turn(strips[1], -8 * m) * has_e,
                              jnp.where(lane >= 120, turn(strips[0], 120 - 8 * m) * has_w, 0.0))
             if there is not None:
@@ -247,7 +308,7 @@
             old[base + i, :, 0:128] = middle
             old[base + i, :, 128:256] = side
     kept = jnp.where(lane < 64, has_e, has_w)
-    stay, cw, ce, cs, cn = stencil(spread * (1.0 / 3.0))
+    stay, cw, ce, cs, cn = factors(spread * (1.0 / 3.0), east_by, north_by)
     new[0] = jnp.zeros((C, PWIDE), F32)
     new[PROWS - 1] = jnp.zeros((C, PWIDE), F32)
 
@@ -299,7 +360,7 @@
                 total = total + jnp.dot(part, hat, preferred_element_type=F32)
             lines[i] = total * (2.0 / 9.0)
 
-    stay, cw, ce, cs, cn = stencil(spread)
+    stay, cw, ce, cs, cn = factors(spread, east_by, north_by)
     second = [lane + 128 * half for half in range(2)]
     second = [(at >= SLOT) & (at < 2 * SLOT) for at in second]
 
@@ -328,7 +389,7 @@
                         + cn * source[y + 1, :, at] + force[C * r : C * r + C, at])
             return carry
 
-        lax.fori_loop(0, (high - low) // CHUNK, body, 0)
+        lax.fori_loop(0, (high - low) // CHUNK, body, 0, unroll=True)
 
         for edge, tile, spot in ((0, 0, 0), (tiles_x - 1, NXD // 128 - 1, 127)):
             @pl.when(gx == edge)
@@ -365,9 +426,9 @@
     step(one, two, push, 1, ROWS - 1, 1)
     for move in moves:
         move.wait()
-    push = thrusts(gathered(two), scale)
+    push = thrusts(gathered(two) + missing[0], scale)
     step(two, one, push, 7, ROWS - 7, 2)
-    push = thrusts(gathered(one), scale)
+    push = thrusts(gathered(one) + missing[1], scale)
     step(one, two, push, 13, ROWS - 13, 3)
 
     stores = [pltpu.make_async_copy(two.at[pl.ds(H, NYD), c, pl.ds(0, NXD)], nest_out.at[c], out_sem.at[c]) for c in range(C)]
@@ -418,26 +479,32 @@
     smem = pl.BlockSpec(memory_space=pltpu.SMEM)
     vmem = pl.BlockSpec(memory_space=pltpu.VMEM)
     anywhere = pl.BlockSpec(memory_space=pl.ANY)
-    passed = ((NYD, C, NXD), (H, C, NXD), (H, C, NXD), (PYD, C, PXD), (PH, C, PXD), (PH, C, PXD),
-              (8, C, 128), (8, C, 128), (4, 4, C, 128), (3, C, 128))
+    passed = ((NYD, C, NXD), (NEAR, C, NXD), (NEAR, C, NXD), (PYD, C, PXD), (PNEAR, C, PXD), (PNEAR, C, PXD),
+              (8, C, 128), (8, C, 128), (4, 4, C, 128), (1, C, 128), (2, 7, C, 128))
 
     def on_device(nest_wind, parent_wind, diffusion, drift, disk_sites, disk_live, disk_coef):
         rims = pl.pallas_call(
             functools.partial(exchange, tiles_x, tiles_y),
             out_shape=[pltpu.VMEM(shape, F32) for shape in passed],
-            in_specs=[anywhere, anywhere, smem, smem, smem],
+            in_specs=[pl.BlockSpec(memory_space=pltpu.HBM)] * 7,
             out_specs=[vmem] * len(passed),
             scratch_shapes=[
+                pltpu.VMEM((24, C, 128), F32),
                 pltpu.VMEM((10, C, 128), F32),
-                pltpu.VMEM((10, C, 128), F32),
-                pltpu.SemaphoreType.DMA((2 * C,)),
+                pltpu.SMEM(diffusion.shape, F32),
+                pltpu.SMEM(drift.shape, F32),
+                pltpu.SMEM((2, 1, 1, MAXD), jnp.int32),
+                pltpu.SMEM((1, 1, MAXD), jnp.int32),
+                pltpu.SMEM((1, 1, MAXD), F32),
+                pltpu.SemaphoreType.DMA((2 * C + 5,)),
                 pltpu.SemaphoreType.DMA((12,)),
                 pltpu.SemaphoreType.DMA((12,)),
             ],
             compiler_params=pltpu.CompilerParams(
                 collective_id=0, has_side_effects=True, vmem_limit_bytes=16 * 2**20),
             name="exchange",
-        )(nest_wind, parent_wind, disk_sites, disk_live, disk_coef)
+        )(*[pltpu.with_memory_space_constraint(x, pltpu.HBM) for x in
+            (nest_wind, parent_wind, diffusion, drift, disk_sites, disk_live, disk_coef)])
         return tuple(pl.pallas_call(
             functools.partial(advance_all, tiles_x, tiles_y),
             out_shape=[jax.ShapeDtypeStruct(nest_wind.shape, F32), jax.ShapeDtypeStruct(parent_wind.shape, F32)],

time: 59.6 us -> 47.2 us (0.79)
  Pallas kernels: 54.3 us -> 46.1 us
  local copies, waits for them, and re-layouts: 4.16 us -> 0.01 us
    pallas_call x1, Pallas kernels: 39.2 us -> 33.3 us  [on_device(): pl.pallas_call(functools.partial(exchange, tiles_x, tiles_y), out_shape=[...]
    unnamed x14 -> x4, local copies, waits for them, and re-layouts: 4.16 us -> 0.01 us
    pallas_call x1, Pallas kernels: 15.2 us -> 12.8 us  [on_device(): pl.pallas_call(functools.partial(advance_all, tiles_x, tiles_y), out_shap...]
where the time goes in v2:
time: 47.2 us; the launch traced here: 46.8 us
  Pallas kernels  46.1 us (98%)
  between operations  0.67 us (1%)
    pallas_call x1, Pallas kernels, on_device(): pl.pallas_call(functools.partial(exchange, tiles_x, tiles_y), out_shape=[...  33.3 us
    pallas_call x1, Pallas kernels, on_device(): pl.pallas_call(functools.partial(advance_all, tiles_x, tiles_y), out_shap...  12.8 us

profile of v2, /device:TPU:24, one launch (start us, length us, event | category | flops | bytes accessed | tf_op | source)
XLA Modules:
  0.0 46.8 jit_solution(11125894181976694489)
XLA Ops:
  0.6 0.0 copy-start
  0.6 0.0 copy-start.1
  0.7 33.3 %exchange.1 = (f32[48,16,384]{2,1,0:T(8,128)S(1)}, f32[6,16,384]{2,1,0:T(8,128)S(1)}, f32[6,16,384]{2,1,0:T(8,128)S(1)}, f32[16,16,128]{2,1,0:T(8,128)S(1)}, f32...) custom-call(f32[16,48,384]{2,1,0:T(8,128)} %nest.1, ...), custom_call_target="tpu_custom_call" | custom-call | tf_op jit(solution)/shard_map/exchange/pallas_call | solution.py:486
  33.9 0.0 copy-done
  33.9 0.0 copy-done.1
  33.9 12.8 %advance.1 = (f32[16,48,384]{2,1,0:T(8,128)}, f32[16,16,128]{2,1,0:T(8,128)}) custom-call(f32[16]{0:T(128)S(1)} %copy-done.1, f32[2,16]{1,0:T(2,128)S(1)} %copy-done, f32[48,16,384]{2,1,0:T(8,128)S(1)} %get-tuple-element.13.own, f32[6,16,384]{2,1,0:T(8,128)S(1)} %get-tuple-element.14.south, f32[6,16,384]{2,1,0:T(8,128)S(1)} %get-tuple-element.15.north, ...), custom_call_target="tpu_custom_call" | custom-call | tf_op jit(solution)/shard_map/advance/pallas_call | solution.py:508
Async XLA Ops:
  0.6 33.3 %copy-start = (f32[2,16]{1,0:T(2,128)S(1)}, f32[2,16]{1,0:T(2,128)}, u32[]{:S(2)}) copy-start(f32[2,16]{1,0:T(2,128)} %drift.1) | copy-start | bytes 388
  0.6 33.3 %copy-start.1 = (f32[16]{0:T(128)S(1)}, f32[16]{0:T(128)}, u32[]{:S(2)}) copy-start(f32[16]{0:T(128)} %diffusion.1) | copy-start | bytes 196

commit v3 on v2

--- a/solution.py
+++ b/solution.py
@@ -61,16 +61,25 @@
 
 
 def exchange(tiles_x, tiles_y, nest, parent, diffusion_h, drift_h, sites_h, live_h, coef_h,
-             own, south, north, pown, psouth, pnorth, west, east, corner, info, sides,
-             pack_w, pack_e, diffusion, drift, sites, live, coef, in_sem, send_sem, recv_sem):
+             own, south, north, pown, psouth, pnorth, west, east, corner, side, notes,
+             pack_w, pack_e, pack_y, own_notes, diffusion, drift, sites, live, coef, in_sem, send_sem, recv_sem):
     gx, gy = lax.axis_index("gx"), lax.axis_index("gy")
 
     def device(dx, dy):
         return (lax.rem(gx + dx + tiles_x, tiles_x), lax.rem(gy + dy + tiles_y, tiles_y))
 
+    def exists(dx, dy):
+        at_x, at_y = gx + dx, gy + dy
+        return (at_x >= 0) & (at_x < tiles_x) & (at_y >= 0) & (at_y < tiles_y)
+
     barrier = pltpu.get_barrier_semaphore()
+    around = 0
     for dx, dy in AROUND[1:]:
-        pl.semaphore_signal(barrier, inc=1, device_id=device(dx, dy), device_id_type=MESH)
+        around = around + exists(dx, dy).astype(jnp.int32)
+
+        @pl.when(exists(dx, dy))
+        def _():
+            pl.semaphore_signal(barrier, inc=1, device_id=device(dx, dy), device_id_type=MESH)
 
     small = ((diffusion_h, diffusion), (drift_h, drift), (sites_h, sites), (live_h, live), (coef_h, coef))
     loads = [pltpu.make_async_copy(nest.at[c], own.at[:, c, :], in_sem.at[c]) for c in range(C)]
@@ -88,16 +97,34 @@
             for j in range(8):
                 cells = own[8 * p + j, :, 128 * tile : 128 * tile + 128]
                 packed = jnp.where(lane // 16 == j, turn(cells, 16 * j - first), packed)
-            pack[2 + p] = packed
-    for pack, first in ((pack_w, 0), (pack_e, 120)):
+            pack[p] = packed
+    for way, base in ((0, 0), (1, NYD - H)):
+        packed = jnp.zeros((C, 128), F32)
+        for i in range(H):
+            packed = jnp.where(lane // 4 == i, turn(own[base + i, :, 0:128], 4 * i), packed)
+            packed = jnp.where(lane // 4 == H + i, turn(own[base + i, :, NXD - 128 : NXD], 4 * i + 64 - 124), packed)
+        pack_y[way] = packed
+    strips = []
+    edge = jnp.where(gy == tiles_y - 1, PYD - 1, 0)
+    after = jnp.where(gy == tiles_y - 1, PYD - 2, 1)
+    for first, wide in ((0, 0), (124, 120)):
         packed = jnp.zeros((C, 128), F32)
         for m in range(PYD):
-            packed = jnp.where(lane // 8 == m, turn(pown[m], 8 * m - first), packed)
-        pack[0] = packed
-        pack[8] = packed
+            packed = jnp.where(lane // 4 == PYD + m, turn(pown[m], 64 + 4 * m - first), packed)
+        packed = jnp.where(lane // 8 == 6, turn(pown[edge], 48 - wide), packed)
+        packed = jnp.where(lane // 8 == 7, turn(pown[after], 56 - wide), packed)
+        strips.append(packed)
+    shores = []
+    for base in (0, PYD - PH):
+        packed = jnp.zeros((C, 128), F32)
+        for i in range(PH):
+            cells = pown[base + i]
+            packed = jnp.where(lane // 2 == 24 + i, jnp.where(
+                gx == 0, turn(cells, 48 + 2 * i), turn(cells, 48 + 2 * i - 126)), packed)
+        shores.append(packed)
 
     wide_lane = lanes_of((C, NXD))
-    inner = (wide_lane >= H) & (wide_lane < NXD - H)
+    inner = (wide_lane >= 4) & (wide_lane < NXD - 4)
     stay, cw, ce, cs, cn = factors(
         plane_tile(lambda c: diffusion[c]), plane_tile(lambda c: drift[0, c]), plane_tile(lambda c: drift[1, c]))
     middle = stay * stay + 2.0 * (cw * ce + cs * cn)
@@ -143,54 +170,55 @@
                     value = value + term * ((row + r >= low) & (row + r <= high)).astype(F32)
                 rests[way] = jnp.where(lane == at, value, rests[way])
     mine = thrusts(wind, scale) + spot
-    info[0] = mine
-    for pack in (pack_w, pack_e):
-        pack[1] = mine
-        pack[9] = mine
-    for way in range(2):
-        base = 10 + 7 * way
-        for i in range(2):
-            first = 2 + i if way == 0 else 6 + i
-            pack_w[base + i] = pack_w[first]
-            pack_w[base + 2 + i] = pack_e[first]
-        pack_w[base + 4] = pack_w[0]
-        pack_w[base + 5] = pack_e[0]
-        pack_w[base + 6] = mine + rests[way]
-
-    sends = (
-        (pack_e.at[pl.ds(6, 4)], corner.at[0], (1, 1)),
-        (pack_w.at[pl.ds(6, 4)], corner.at[1], (-1, 1)),
-        (pack_e.at[pl.ds(0, 4)], corner.at[2], (1, -1)),
-        (pack_w.at[pl.ds(0, 4)], corner.at[3], (-1, -1)),
-        (pack_e.at[pl.ds(0, 8)], west, (1, 0)),
-        (pack_w.at[pl.ds(0, 8)], east, (-1, 0)),
+    notes[0] = mine
+    for i, extra in enumerate((rests[0] + shores[0], rests[1] + shores[1], strips[0], strips[1])):
+        own_notes[i] = mine + extra
+
+    for dx, dy, buffers in (
+        (0, -1, (south, psouth, side.at[0])), (0, 1, (north, pnorth, side.at[1])), (-1, 0, (west,)), (1, 0, (east,)),
+        (-1, -1, (corner.at[0],)), (1, -1, (corner.at[1],)), (-1, 1, (corner.at[2],)), (1, 1, (corner.at[3],)),
+    ):
+        @pl.when(jnp.logical_not(exists(dx, dy)))
+        def _():
+            for buffer in buffers + (notes.at[AROUND.index((dx, dy))],):
+                buffer[...] = jnp.zeros(buffer.shape, F32)
+
+    sends = [(own_notes.at[0 if dy < 0 else 1] if dx == 0 else own_notes.at[2 if dx < 0 else 3],
+              notes.at[AROUND.index((-dx, -dy))], (dx, dy)) for dx, dy in AROUND[:0:-1]]
+    sends += [
+        (pack_e.at[pl.ds(4, 2)], corner.at[0], (1, 1)),
+        (pack_w.at[pl.ds(4, 2)], corner.at[1], (-1, 1)),
+        (pack_e.at[pl.ds(0, 2)], corner.at[2], (1, -1)),
+        (pack_w.at[pl.ds(0, 2)], corner.at[3], (-1, -1)),
+        (pack_e, west, (1, 0)),
+        (pack_w, east, (-1, 0)),
         (own.at[pl.ds(NYD - NEAR, NEAR)], south, (0, 1)),
         (own.at[pl.ds(0, NEAR)], north, (0, -1)),
         (pown.at[pl.ds(PYD - PNEAR, PNEAR)], psouth, (0, 1)),
         (pown.at[pl.ds(0, PNEAR)], pnorth, (0, -1)),
-        (pack_w.at[pl.ds(17, 7)], sides.at[0], (0, 1)),
-        (pack_w.at[pl.ds(10, 7)], sides.at[1], (0, -1)),
-    )
-    pl.semaphore_wait(barrier, len(AROUND) - 1)
+        (pack_y.at[1], side.at[0], (0, 1)),
+        (pack_y.at[0], side.at[1], (0, -1)),
+    ]
+    pl.semaphore_wait(barrier, around)
     copies = []
     for i, (source, target, (dx, dy)) in enumerate(sends):
         copy = pltpu.make_async_remote_copy(
             src_ref=source, dst_ref=target, send_sem=send_sem.at[i], recv_sem=recv_sem.at[i],
             device_id=device(dx, dy), device_id_type=MESH,
         )
-        copy.start()
-        copies.append(copy)
-    for copy in copies:
-        copy.wait()
-
-
-def advance_all(tiles_x, tiles_y, diffusion, drift, own, south, north, pown, psouth, pnorth, west, east, corner, info, sides,
+        copies.append((copy, exists(dx, dy), exists(-dx, -dy)))
+        pl.when(exists(dx, dy))(copy.start)
+    for copy, sent, received in copies:
+        pl.when(sent)(copy.wait_send)
+        pl.when(received)(copy.wait_recv)
+
+
+def advance_all(tiles_x, tiles_y, diffusion, drift, own, south, north, pown, psouth, pnorth, west, east, corner, side, note_in,
                 nest_out, parent_out,
                 one, two, old, new, cols_old, cols_new, lines, row_g, col_g, places, out_v, sum_v, place_sem, out_sem):
     gx, gy = lax.axis_index("gx"), lax.axis_index("gy")
     lane = lanes_of((C, 128))
-    notes = (info.at[0], sides.at[0, 6], sides.at[1, 6], west.at[1], east.at[1],
-             corner.at[0, 3], corner.at[1, 3], corner.at[2, 1], corner.at[3, 1])
+    notes = [note_in.at[j] for j in range(9)]
     moves = [pltpu.make_async_copy(note.at[pl.ds(0, 8)], places.at[j], place_sem.at[j]) for j, note in enumerate(notes)]
     for move in moves:
         move.start()
@@ -261,18 +289,18 @@
         if p < 2:
             from_w, from_e = corner[0, p], corner[1, p]
         elif p < 8:
-            from_w, from_e = west[p], east[p]
+            from_w, from_e = west[p - 2], east[p - 2]
         else:
-            from_w, from_e = corner[2, p - 6], corner[3, p - 6]
+            from_w, from_e = corner[2, p - 8], corner[3, p - 8]
         for j in range(8):
             y = 8 * p + j
             one[y, :, NXD:WIDE] = jnp.where(
                 lane < 16, turn(from_e, -16 * j), jnp.where(lane >= 112, turn(from_w, 112 - 16 * j), 0.0))
             if y < H - NEAR or y >= H + NYD + NEAR:
-                way, i = (0, p) if y < H else (1, p - 8)
-                one[y, :, 0:128] = jnp.where(lane < 16, turn(sides[way, i], -16 * j), 0.0)
+                way, i = (0, y) if y < H else (1, y - H - NYD)
+                one[y, :, 0:128] = jnp.where(lane < 4, turn(side[way], -4 * i), 0.0)
                 one[y, :, 128 : NXD - 128] = jnp.zeros((C, NXD - 256), F32)
-                one[y, :, NXD - 128 : NXD] = jnp.where(lane >= 112, turn(sides[way, 2 + i], 112 - 16 * j), 0.0)
+                one[y, :, NXD - 128 : NXD] = jnp.where(lane >= 124, turn(side[way], 60 - 4 * i), 0.0)
 
     spread = plane_tile(lambda c: diffusion[c])
     east_by = plane_tile(lambda c: drift[0, c])
@@ -286,27 +314,29 @@
         from_e = [jnp.where(lane == 127, down[(t + 1) % count], down[t]) for t in range(count)]
         return from_w, from_e
 
-    for block, (source, there, strips) in enumerate((
-        (psouth, has_s, (corner[0, 2], corner[1, 2], 8)),
-        (pown, None, (west[0], east[0], 0)),
-        (pnorth, has_n, (corner[2, 0], corner[3, 0], 0)),
+    for block, (source, strip_w, strip_e, base, first, count) in enumerate((
+        (psouth, note_in[5], note_in[6], 0, PH, PH),
+        (pown, note_in[3], note_in[4], PH, 0, PYD),
+        (pnorth, note_in[7], note_in[8], PH + PYD, 0, PH),
     )):
-        base = (0, PH, PH + PYD)[block]
-        count = (PH, PYD, PH)[block]
         for i in range(count):
-            m = i + strips[2]
+            m = first + i
             if block == 0 and i < PH - PNEAR or block == 2 and i >= PNEAR:
-                way = block // 2
-                middle = jnp.where(lane < 8, turn(sides[way, 4], -8 * m),
-                                   jnp.where(lane >= 120, turn(sides[way, 5], 120 - 8 * m), 0.0))
+                shore = note_in[1 + block // 2]
+                middle = jnp.where((lane < 2) & (gx == 0), turn(shore, -48 - 2 * i),
+                                   jnp.where((lane >= 126) & (gx == tiles_x - 1), turn(shore, 78 - 2 * i), 0.0))
             else:
                 middle = source[i - (PH - PNEAR) if block == 0 else i]
-            side = jnp.where(lane < 8, turn(strips[1], -8 * m) * has_e,
-                             jnp.where(lane >= 120, turn(strips[0], 120 - 8 * m) * has_w, 0.0))
-            if there is not None:
-                middle, side = middle * there, side * there
             old[base + i, :, 0:128] = middle
-            old[base + i, :, 128:256] = side
+            old[base + i, :, 128:256] = jnp.where(
+                lane < 4, turn(strip_e, -64 - 4 * m), jnp.where(lane >= 124, turn(strip_w, 60 - 4 * m), 0.0))
+
+    @pl.when((gy == 0) | (gy == tiles_y - 1))
+    def _():
+        for i, at in enumerate((jnp.where(gy == 0, PH, PH + PYD - 1), jnp.where(gy == 0, PH + 1, PH + PYD - 2))):
+            old[at, :, 128:256] = jnp.where(lane < 8, turn(note_in[4], -48 - 8 * i), jnp.where(
+                lane >= 120, turn(note_in[3], 72 - 8 * i), 0.0))
+
     kept = jnp.where(lane < 64, has_e, has_w)
     stay, cw, ce, cs, cn = factors(spread * (1.0 / 3.0), east_by, north_by)
     new[0] = jnp.zeros((C, PWIDE), F32)
@@ -480,7 +510,7 @@
     vmem = pl.BlockSpec(memory_space=pltpu.VMEM)
     anywhere = pl.BlockSpec(memory_space=pl.ANY)
     passed = ((NYD, C, NXD), (NEAR, C, NXD), (NEAR, C, NXD), (PYD, C, PXD), (PNEAR, C, PXD), (PNEAR, C, PXD),
-              (8, C, 128), (8, C, 128), (4, 4, C, 128), (1, C, 128), (2, 7, C, 128))
+              (6, C, 128), (6, C, 128), (4, 2, C, 128), (2, C, 128), (9, C, 128))
 
     def on_device(nest_wind, parent_wind, diffusion, drift, disk_sites, disk_live, disk_coef):
         rims = pl.pallas_call(
@@ -489,16 +519,18 @@
             in_specs=[pl.BlockSpec(memory_space=pltpu.HBM)] * 7,
             out_specs=[vmem] * len(passed),
             scratch_shapes=[
-                pltpu.VMEM((24, C, 128), F32),
-                pltpu.VMEM((10, C, 128), F32),
+                pltpu.VMEM((6, C, 128), F32),
+                pltpu.VMEM((6, C, 128), F32),
+                pltpu.VMEM((2, C, 128), F32),
+                pltpu.VMEM((4, C, 128), F32),
                 pltpu.SMEM(diffusion.shape, F32),
                 pltpu.SMEM(drift.shape, F32),
                 pltpu.SMEM((2, 1, 1, MAXD), jnp.int32),
                 pltpu.SMEM((1, 1, MAXD), jnp.int32),
                 pltpu.SMEM((1, 1, MAXD), F32),
                 pltpu.SemaphoreType.DMA((2 * C + 5,)),
-                pltpu.SemaphoreType.DMA((12,)),
-                pltpu.SemaphoreType.DMA((12,)),
+                pltpu.SemaphoreType.DMA((20,)),
+                pltpu.SemaphoreType.DMA((20,)),
             ],
             compiler_params=pltpu.CompilerParams(
                 collective_id=0, has_side_effects=True, vmem_limit_bytes=16 * 2**20),

time: 47.2 us -> 41.5 us (0.88)
  the two profiles are of different devices: /device:TPU:24 before, /device:TPU:30 now
where the time goes in v3:
time: 41.5 us; the launch traced here: 41.3 us
  Pallas kernels  40.7 us (98%)
  between operations  0.67 us (2%)
    pallas_call x1, Pallas kernels, on_device(): pl.pallas_call(functools.partial(exchange, tiles_x, tiles_y), out_shape=[...  29.2 us
    pallas_call x1, Pallas kernels, on_device(): pl.pallas_call(functools.partial(advance_all, tiles_x, tiles_y), out_shap...  11.5 us

profile of v3, /device:TPU:30, one launch (start us, length us, event | category | flops | bytes accessed | tf_op | source)
XLA Modules:
  0.0 41.3 jit_solution(160571263576231432)
XLA Ops:
  0.6 0.0 copy-start
  0.6 0.0 copy-start.1
  0.7 29.2 %exchange.1 = (f32[48,16,384]{2,1,0:T(8,128)S(1)}, f32[6,16,384]{2,1,0:T(8,128)S(1)}, f32[6,16,384]{2,1,0:T(8,128)S(1)}, f32[16,16,128]{2,1,0:T(8,128)S(1)}, f32...) custom-call(f32[16,48,384]{2,1,0:T(8,128)} %nest.1, ...), custom_call_target="tpu_custom_call" | custom-call | tf_op jit(solution)/shard_map/exchange/pallas_call | solution.py:516
  29.8 0.0 copy-done
  29.9 0.0 copy-done.1
  29.9 11.5 %advance.1 = (f32[16,48,384]{2,1,0:T(8,128)}, f32[16,16,128]{2,1,0:T(8,128)}) custom-call(f32[16]{0:T(128)S(1)} %copy-done.1, f32[2,16]{1,0:T(2,128)S(1)} %copy-done, f32[48,16,384]{2,1,0:T(8,128)S(1)} %get-tuple-element.13.own, f32[6,16,384]{2,1,0:T(8,128)S(1)} %get-tuple-element.14.south, f32[6,16,384]{2,1,0:T(8,128)S(1)} %get-tuple-element.15.north, ...), custom_call_target="tpu_custom_call" | custom-call | tf_op jit(solution)/shard_map/advance/pallas_call | solution.py:540
Async XLA Ops:
  0.6 29.2 %copy-start = (f32[2,16]{1,0:T(2,128)S(1)}, f32[2,16]{1,0:T(2,128)}, u32[]{:S(2)}) copy-start(f32[2,16]{1,0:T(2,128)} %drift.1) | copy-start | bytes 388
  0.6 29.2 %copy-start.1 = (f32[16]{0:T(128)S(1)}, f32[16]{0:T(128)}, u32[]{:S(2)}) copy-start(f32[16]{0:T(128)} %diffusion.1) | copy-start | bytes 196

commit v4 on v3

--- a/solution.py
+++ b/solution.py
@@ -60,9 +60,51 @@
     return (1.0 - 4.0 * spread - east_by - north_by, spread + east_by, spread, spread + north_by, spread)
 
 
+def shifted(tiles):
+    lane = lanes_of((C, 128))
+    count = len(tiles)
+    up = [turn(v, 1) for v in tiles]
+    down = [turn(v, -1) for v in tiles]
+    from_w = [jnp.where(lane == 0, up[(t - 1) % count], up[t]) for t in range(count)]
+    from_e = [jnp.where(lane == 127, down[(t + 1) % count], down[t]) for t in range(count)]
+    return from_w, from_e
+
+
+def pieces(value, count):
+    out = []
+    for _ in range(count):
+        part = value.astype(BF16)
+        out.append(part)
+        value = value - part.astype(F32)
+    return out
+
+
+def thrice(value):
+    shape = value.shape
+    at = lanes_of(shape)
+    later = turn(value, SLOT)
+    return (jnp.where(at < SLOT, value, later),
+            jnp.where(at < 2 * SLOT - 128, later, turn(value, 2 * SLOT - 128)))
+
+
+def force_rows(amounts_2, row_g, col_g, base):
+    at = lanes_of((C, 128))
+    second = (at >= SLOT, at < 2 * SLOT - 128)
+    left = []
+    for r in range(CHUNK):
+        halves = []
+        for half in range(2):
+            value = amounts_2[half] * row_g[base + r, :, 128 * half : 128 * half + 128]
+            rest = value - value.astype(BF16).astype(F32)
+            halves.append(jnp.where(second[half], rest, value).astype(BF16))
+        left.append(jnp.concatenate(halves, axis=1))
+    return jnp.dot(jnp.concatenate(left, axis=0), col_g[...], preferred_element_type=F32)
+
+
 def exchange(tiles_x, tiles_y, nest, parent, diffusion_h, drift_h, sites_h, live_h, coef_h,
-             own, south, north, pown, psouth, pnorth, west, east, corner, side, notes,
-             pack_w, pack_e, pack_y, own_notes, diffusion, drift, sites, live, coef, in_sem, send_sem, recv_sem):
+             own, south, north, west, east, corner, side, notes,
+             two, new, cols_old, cols_new, lines, row_g, col_g, scale_out, missing_out, weight_out,
+             pown, psouth, pnorth, old, pack_w, pack_e, pack_y, own_notes, diffusion, drift, sites, live, coef, in_sem, send_sem, recv_sem):
     gx, gy = lax.axis_index("gx"), lax.axis_index("gy")
 
     def device(dx, dy):
@@ -125,8 +167,11 @@
 
     wide_lane = lanes_of((C, NXD))
     inner = (wide_lane >= 4) & (wide_lane < NXD - 4)
+    spread = plane_tile(lambda c: diffusion[c])
+    east_by = plane_tile(lambda c: drift[0, c])
+    north_by = plane_tile(lambda c: drift[1, c])
     stay, cw, ce, cs, cn = factors(
-        plane_tile(lambda c: diffusion[c]), plane_tile(lambda c: drift[0, c]), plane_tile(lambda c: drift[1, c]))
+        spread, east_by, north_by)
     middle = stay * stay + 2.0 * (cw * ce + cs * cn)
 
     def three(value):
@@ -186,6 +231,8 @@
     sends = [(own_notes.at[0 if dy < 0 else 1] if dx == 0 else own_notes.at[2 if dx < 0 else 3],
               notes.at[AROUND.index((-dx, -dy))], (dx, dy)) for dx, dy in AROUND[:0:-1]]
     sends += [
+        (pown.at[pl.ds(PYD - PNEAR, PNEAR)], psouth, (0, 1)),
+        (pown.at[pl.ds(0, PNEAR)], pnorth, (0, -1)),
         (pack_e.at[pl.ds(4, 2)], corner.at[0], (1, 1)),
         (pack_w.at[pl.ds(4, 2)], corner.at[1], (-1, 1)),
         (pack_e.at[pl.ds(0, 2)], corner.at[2], (1, -1)),
@@ -194,8 +241,6 @@
         (pack_w, east, (-1, 0)),
         (own.at[pl.ds(NYD - NEAR, NEAR)], south, (0, 1)),
         (own.at[pl.ds(0, NEAR)], north, (0, -1)),
-        (pown.at[pl.ds(PYD - PNEAR, PNEAR)], psouth, (0, 1)),
-        (pown.at[pl.ds(0, PNEAR)], pnorth, (0, -1)),
         (pack_y.at[1], side.at[0], (0, 1)),
         (pack_y.at[0], side.at[1], (0, -1)),
     ]
@@ -208,21 +253,34 @@
         )
         copies.append((copy, exists(dx, dy), exists(-dx, -dy)))
         pl.when(exists(dx, dy))(copy.start)
-    for copy, sent, received in copies:
-        pl.when(sent)(copy.wait_send)
+    def own_row(i, carry):
+        tiles = [own[i, :, 128 * t : 128 * t + 128] for t in range(3)]
+        up = [turn(v, 1) for v in tiles]
+        down = [turn(v, -1) for v in tiles]
+        below, above = own[jnp.maximum(i - 1, 0)], own[jnp.minimum(i + 1, NYD - 1)]
+        below_by = cs * (i > 0).astype(F32)
+        above_by = cn * (i < NYD - 1).astype(F32)
+        for t in range(3):
+            from_w = jnp.where(lane == 0, up[t - 1] if t > 0 else 0.0, up[t])
+            from_e = jnp.where(lane == 127, down[t + 1] if t < 2 else 0.0, down[t])
+            at = slice(128 * t, 128 * t + 128)
+            two[H + i, :, at] = (stay * tiles[t] + cw * from_w + ce * from_e
+                                 + below_by * below[:, at] + above_by * above[:, at])
+        two[H + i, :, NXD:WIDE] = jnp.where(lane == 0, cw * up[2], jnp.where(lane == 127, ce * down[0], 0.0))
+        return carry
+
+    lax.fori_loop(0, NYD, own_row, 0, unroll=4)
+
+    def clear(i, carry):
+        two[i] = jnp.zeros((C, WIDE), F32)
+        two[H + NYD + i] = jnp.zeros((C, WIDE), F32)
+        return carry
+
+    lax.fori_loop(0, H, clear, 0)
+
+    early = len(AROUND) + 1
+    for copy, sent, received in copies[:early]:
         pl.when(received)(copy.wait_recv)
-
-
-def advance_all(tiles_x, tiles_y, diffusion, drift, own, south, north, pown, psouth, pnorth, west, east, corner, side, note_in,
-                nest_out, parent_out,
-                one, two, old, new, cols_old, cols_new, lines, row_g, col_g, places, out_v, sum_v, place_sem, out_sem):
-    gx, gy = lax.axis_index("gx"), lax.axis_index("gy")
-    lane = lanes_of((C, 128))
-    notes = [note_in.at[j] for j in range(9)]
-    moves = [pltpu.make_async_copy(note.at[pl.ds(0, 8)], places.at[j], place_sem.at[j]) for j, note in enumerate(notes)]
-    for move in moves:
-        move.start()
-
     has_w, has_e = (gx > 0).astype(F32), (gx < tiles_x - 1).astype(F32)
     has_s, has_n = (gy > 0).astype(F32), (gy < tiles_y - 1).astype(F32)
     of_x = {-1: has_w, 0: None, 1: has_e}
@@ -234,7 +292,7 @@
     disk_cols = jnp.full((C, 128), 1.0e6, F32)
     missing = [jnp.zeros((C, 128), F32)] * 2
     for j, (dx, dy) in enumerate(AROUND):
-        note = notes[j][...]
+        note = notes[j]
         here = lane // MAXD == j
         first, force = turn(note, MAXD * j), turn(note, MAXD * j - 3 * MAXD)
         for there in (of_x[dx], of_y[dy]):
@@ -246,13 +304,6 @@
         scale = jnp.where(here, force, scale)
         disk_rows = jnp.where(here, turn(note, MAXD * j - MAXD) + float(H + NYD * dy), disk_rows)
         disk_cols = jnp.where(here, turn(note, MAXD * j - 2 * MAXD) + float(NXD * dx), disk_cols)
-
-    def thrice(value):
-        shape = value.shape
-        at = lanes_of(shape)
-        later = turn(value, SLOT)
-        return (jnp.where(at < SLOT, value, later),
-                jnp.where(at < 2 * SLOT - 128, later, turn(value, 2 * SLOT - 128)))
 
     def profile(distance):
         return jnp.where(jnp.abs(distance) <= float(FOOT), jnp.exp(distance * distance * (-1.0 / 8.0)), 0.0)
@@ -275,6 +326,115 @@
             value = profile(at - across)
             rest = value - value.astype(BF16).astype(F32)
             col_g[128 * half : 128 * half + 128, 128 * tile : 128 * tile + 128] = jnp.where(third, rest, value).astype(BF16)
+    scale_out[...] = scale
+    for i in range(2):
+        missing_out[i] = missing[i]
+
+    low_side = jnp.where(gx == 0, 0, -64)
+    high_side = jnp.where(gx == tiles_x - 1, NXD, NXD + 64)
+    fine = lax.broadcasted_iota(jnp.int32, (WIDE, 128), 0)
+    fine = jnp.where(fine < 448, fine, fine - WIDE)
+    gap = jnp.abs(fine - (3 * lanes_of((WIDE, 128)) + 1))
+    weight = jnp.where(gap <= 1, 2.0, jnp.where(gap <= 4, 1.0, 0.0))
+    weight_out[...] = jnp.where((fine >= low_side) & (fine < high_side), weight, 0.0).astype(BF16)
+
+    for block, (source, strip_w, strip_e, base, first, count) in enumerate((
+        (psouth, notes[5], notes[6], 0, PH, PH),
+        (pown, notes[3], notes[4], PH, 0, PYD),
+        (pnorth, notes[7], notes[8], PH + PYD, 0, PH),
+    )):
+        for i in range(count):
+            m = first + i
+            if block == 0 and i < PH - PNEAR or block == 2 and i >= PNEAR:
+                shore = notes[1 + block // 2]
+                middle = jnp.where((lane < 2) & (gx == 0), turn(shore, -48 - 2 * i),
+                                   jnp.where((lane >= 126) & (gx == tiles_x - 1), turn(shore, 78 - 2 * i), 0.0))
+            else:
+                middle = source[i - (PH - PNEAR) if block == 0 else i]
+            old[base + i, :, 0:128] = middle
+            old[base + i, :, 128:256] = jnp.where(
+                lane < 4, turn(strip_e, -64 - 4 * m), jnp.where(lane >= 124, turn(strip_w, 60 - 4 * m), 0.0))
+
+    @pl.when((gy == 0) | (gy == tiles_y - 1))
+    def _():
+        for i, at in enumerate((jnp.where(gy == 0, PH, PH + PYD - 1), jnp.where(gy == 0, PH + 1, PH + PYD - 2))):
+            old[at, :, 128:256] = jnp.where(lane < 8, turn(notes[4], -48 - 8 * i), jnp.where(
+                lane >= 120, turn(notes[3], 72 - 8 * i), 0.0))
+
+    kept = jnp.where(lane < 64, has_e, has_w)
+    stay, cw, ce, cs, cn = factors(spread * (1.0 / 3.0), east_by, north_by)
+    new[0] = jnp.zeros((C, PWIDE), F32)
+    new[PROWS - 1] = jnp.zeros((C, PWIDE), F32)
+
+    def parent_row(i, carry):
+        inside = jnp.where(i < PH, has_s, jnp.where(i >= PH + PYD, has_n, 1.0))
+        tiles = [old[i, :, 128 * t : 128 * t + 128] for t in range(2)]
+        from_w, from_e = shifted(tiles)
+        for t in range(2):
+            value = (stay * tiles[t] + cw * from_w[t] + ce * from_e[t]
+                     + cs * old[i - 1, :, 128 * t : 128 * t + 128] + cn * old[i + 1, :, 128 * t : 128 * t + 128])
+            value = value * inside
+            new[i, :, 128 * t : 128 * t + 128] = value * kept if t == 1 else value
+        return carry
+
+    lax.fori_loop(1, PROWS - 1, parent_row, 0)
+
+    @pl.when((gx == 0) | (gx == tiles_x - 1))
+    def _():
+        for source, target in ((old, cols_old), (new, cols_new)):
+            for y in range(ROWS):
+                q, rest = (y - H) // 3 + PH, (y - H) % 3
+                centre = source[q, :, 0:128]
+                if rest == 1:
+                    value = centre * (2.0 / 3.0)
+                else:
+                    value = centre * (4.0 / 9.0) + source[q - 1 if rest == 0 else q + 1, :, 0:128] * (2.0 / 9.0)
+                target[y] = value
+
+    @pl.when((gy == 0) | (gy == tiles_y - 1))
+    def _():
+        fine = lanes_of((PWIDE, WIDE))
+        fine = jnp.where(fine < 448, fine, fine - WIDE)
+        coarse = lax.broadcasted_iota(jnp.int32, (PWIDE, WIDE), 0)
+        coarse = jnp.where(coarse < 192, coarse, coarse - PWIDE)
+        hat = jnp.maximum(3 - jnp.abs(fine - (3 * coarse + 1)), 0).astype(F32).astype(BF16)
+        at = jnp.where(gy == 0, PH, PH + PYD - 1)
+        parts = pieces(old[at], 3) + pieces(new[at], 3)
+        for i in range(2):
+            total = jnp.zeros((C, WIDE), F32)
+            for part in parts[3 * i : 3 * i + 3]:
+                total = total + jnp.dot(part, hat, preferred_element_type=F32)
+            lines[i] = total * (2.0 / 9.0)
+
+    amounts_2 = thrice(push)
+
+    def first_force(i, carry):
+        base = 1 + CHUNK * i
+        force = force_rows(amounts_2, row_g, col_g, base)
+        for r in range(CHUNK):
+            two[base + r] += force[C * r : C * r + C]
+        return carry
+
+    lax.fori_loop(0, (ROWS - 2) // CHUNK, first_force, 0)
+
+    for i, (copy, sent, received) in enumerate(copies):
+        pl.when(sent)(copy.wait_send)
+        if i >= early:
+            pl.when(received)(copy.wait_recv)
+
+
+def advance_all(tiles_x, tiles_y, diffusion, drift, own, south, north, west, east, corner, side, note_in,
+                begun, new, cols_old, cols_new, lines, row_g, col_g, scale_in, missing, weight_in,
+                nest_out, parent_out,
+                one, two, places, out_v, sum_v, place_sem, out_sem):
+    gx, gy = lax.axis_index("gx"), lax.axis_index("gy")
+    lane = lanes_of((C, 128))
+    notes = [note_in.at[j] for j in range(9)]
+    moves = [pltpu.make_async_copy(note.at[pl.ds(0, 8)], places.at[j], place_sem.at[j]) for j, note in enumerate(notes)]
+    for move in moves:
+        move.start()
+    has_s, has_n = (gy > 0).astype(F32), (gy < tiles_y - 1).astype(F32)
+    scale = scale_in[...]
 
     def copy_rows(source, base, count):
         def body(i, carry):
@@ -283,7 +443,8 @@
         lax.fori_loop(0, count, body, 0)
 
     copy_rows(south, H - NEAR, NEAR)
-    copy_rows(own, H, NYD)
+    one[H, :, 0:NXD] = own[0]
+    one[H + NYD - 1, :, 0:NXD] = own[NYD - 1]
     copy_rows(north, H + NYD, NEAR)
     for p in range(ROWS // 8):
         if p < 2:
@@ -306,121 +467,47 @@
     east_by = plane_tile(lambda c: drift[0, c])
     north_by = plane_tile(lambda c: drift[1, c])
 
-    def shifted(tiles):
-        count = len(tiles)
-        up = [turn(v, 1) for v in tiles]
-        down = [turn(v, -1) for v in tiles]
-        from_w = [jnp.where(lane == 0, up[(t - 1) % count], up[t]) for t in range(count)]
-        from_e = [jnp.where(lane == 127, down[(t + 1) % count], down[t]) for t in range(count)]
-        return from_w, from_e
-
-    for block, (source, strip_w, strip_e, base, first, count) in enumerate((
-        (psouth, note_in[5], note_in[6], 0, PH, PH),
-        (pown, note_in[3], note_in[4], PH, 0, PYD),
-        (pnorth, note_in[7], note_in[8], PH + PYD, 0, PH),
-    )):
-        for i in range(count):
-            m = first + i
-            if block == 0 and i < PH - PNEAR or block == 2 and i >= PNEAR:
-                shore = note_in[1 + block // 2]
-                middle = jnp.where((lane < 2) & (gx == 0), turn(shore, -48 - 2 * i),
-                                   jnp.where((lane >= 126) & (gx == tiles_x - 1), turn(shore, 78 - 2 * i), 0.0))
-            else:
-                middle = source[i - (PH - PNEAR) if block == 0 else i]
-            old[base + i, :, 0:128] = middle
-            old[base + i, :, 128:256] = jnp.where(
-                lane < 4, turn(strip_e, -64 - 4 * m), jnp.where(lane >= 124, turn(strip_w, 60 - 4 * m), 0.0))
-
-    @pl.when((gy == 0) | (gy == tiles_y - 1))
-    def _():
-        for i, at in enumerate((jnp.where(gy == 0, PH, PH + PYD - 1), jnp.where(gy == 0, PH + 1, PH + PYD - 2))):
-            old[at, :, 128:256] = jnp.where(lane < 8, turn(note_in[4], -48 - 8 * i), jnp.where(
-                lane >= 120, turn(note_in[3], 72 - 8 * i), 0.0))
-
-    kept = jnp.where(lane < 64, has_e, has_w)
-    stay, cw, ce, cs, cn = factors(spread * (1.0 / 3.0), east_by, north_by)
-    new[0] = jnp.zeros((C, PWIDE), F32)
-    new[PROWS - 1] = jnp.zeros((C, PWIDE), F32)
-
-    def parent_row(i, carry):
-        inside = jnp.where(i < PH, has_s, jnp.where(i >= PH + PYD, has_n, 1.0))
-        tiles = [old[i, :, 128 * t : 128 * t + 128] for t in range(2)]
+    stay, cw, ce, cs, cn = factors(spread, east_by, north_by)
+    def swept(source, y):
+        tiles = [source[y, :, 128 * t : 128 * t + 128] for t in range(4)]
         from_w, from_e = shifted(tiles)
-        for t in range(2):
-            value = (stay * tiles[t] + cw * from_w[t] + ce * from_e[t]
-                     + cs * old[i - 1, :, 128 * t : 128 * t + 128] + cn * old[i + 1, :, 128 * t : 128 * t + 128])
-            value = value * inside
-            new[i, :, 128 * t : 128 * t + 128] = value * kept if t == 1 else value
-        return carry
-
-    lax.fori_loop(1, PROWS - 1, parent_row, 0)
-
-    @pl.when((gx == 0) | (gx == tiles_x - 1))
-    def _():
-        for source, target in ((old, cols_old), (new, cols_new)):
-            for y in range(ROWS):
-                q, rest = (y - H) // 3 + PH, (y - H) % 3
-                centre = source[q, :, 0:128]
-                if rest == 1:
-                    value = centre * (2.0 / 3.0)
-                else:
-                    value = centre * (4.0 / 9.0) + source[q - 1 if rest == 0 else q + 1, :, 0:128] * (2.0 / 9.0)
-                target[y] = value
-
-    def pieces(value, count):
         out = []
-        for _ in range(count):
-            part = value.astype(BF16)
-            out.append(part)
-            value = value - part.astype(F32)
+        for t in range(4):
+            at = slice(128 * t, 128 * t + 128)
+            out.append(stay * tiles[t] + cw * from_w[t] + ce * from_e[t]
+                       + cs * source[y - 1, :, at] + cn * source[y + 1, :, at])
         return out
 
-    @pl.when((gy == 0) | (gy == tiles_y - 1))
-    def _():
-        fine = lanes_of((PWIDE, WIDE))
-        fine = jnp.where(fine < 448, fine, fine - WIDE)
-        coarse = lax.broadcasted_iota(jnp.int32, (PWIDE, WIDE), 0)
-        coarse = jnp.where(coarse < 192, coarse, coarse - PWIDE)
-        hat = jnp.maximum(3 - jnp.abs(fine - (3 * coarse + 1)), 0).astype(F32).astype(BF16)
-        at = jnp.where(gy == 0, PH, PH + PYD - 1)
-        parts = pieces(old[at], 3) + pieces(new[at], 3)
-        for i in range(2):
-            total = jnp.zeros((C, WIDE), F32)
-            for part in parts[3 * i : 3 * i + 3]:
-                total = total + jnp.dot(part, hat, preferred_element_type=F32)
-            lines[i] = total * (2.0 / 9.0)
-
-    stay, cw, ce, cs, cn = factors(spread, east_by, north_by)
-    second = [lane + 128 * half for half in range(2)]
-    second = [(at >= SLOT) & (at < 2 * SLOT) for at in second]
-
-    def step(source, target, amounts, low, high, k):
-        amounts_2 = thrice(amounts)
-
-        def body(i, carry):
-            base = low + CHUNK * i
-            left = []
-            for r in range(CHUNK):
-                halves = []
-                for half in range(2):
-                    value = amounts_2[half] * row_g[base + r, :, 128 * half : 128 * half + 128]
-                    rest = value - value.astype(BF16).astype(F32)
-                    halves.append(jnp.where(second[half], rest, value).astype(BF16))
-                left.append(jnp.concatenate(halves, axis=1))
-            force = jnp.dot(jnp.concatenate(left, axis=0), col_g[...], preferred_element_type=F32)
-            for r in range(CHUNK):
-                y = base + r
-                tiles = [source[y, :, 128 * t : 128 * t + 128] for t in range(4)]
-                from_w, from_e = shifted(tiles)
-                for t in range(4):
+    def finish_first():
+        def frame(i, carry):
+            for y in (1 + i, H + NYD + i):
+                for t, value in enumerate(swept(one, y)):
                     at = slice(128 * t, 128 * t + 128)
-                    target[y, :, at] = (
-                        stay * tiles[t] + cw * from_w[t] + ce * from_e[t] + cs * source[y - 1, :, at]
-                        + cn * source[y + 1, :, at] + force[C * r : C * r + C, at])
+                    two[y, :, at] = begun[y, :, at] + value
             return carry
 
-        lax.fori_loop(0, (high - low) // CHUNK, body, 0, unroll=True)
-
+        lax.fori_loop(0, H - 1, frame, 0, unroll=3)
+
+        def inside(i, carry):
+            y = H + i
+            tile = one[y, :, NXD:WIDE]
+            up, down = turn(tile, 1), turn(tile, -1)
+            two[y, :, 0:128] = begun[y, :, 0:128] + jnp.where(lane == 0, cw * up, 0.0)
+            two[y, :, 128:256] = begun[y, :, 128:256]
+            two[y, :, 256:384] = begun[y, :, 256:384] + jnp.where(lane == 127, ce * down, 0.0)
+            two[y, :, NXD:WIDE] = (
+                begun[y, :, NXD:WIDE] + stay * tile + jnp.where(lane == 0, 0.0, cw * up)
+                + jnp.where(lane == 127, 0.0, ce * down) + cs * one[y - 1, :, NXD:WIDE] + cn * one[y + 1, :, NXD:WIDE])
+            return carry
+
+        lax.fori_loop(0, NYD, inside, 0, unroll=6)
+        for y, by, beyond in ((H, cs, H - 1), (H + NYD - 1, cn, H + NYD)):
+            for t in range(3):
+                at = slice(128 * t, 128 * t + 128)
+                two[y, :, at] += by * one[beyond, :, at]
+        hold_edges(two, 1, ROWS - 1, 1)
+
+    def hold_edges(target, low, high, k):
         for edge, tile, spot in ((0, 0, 0), (tiles_x - 1, NXD // 128 - 1, 127)):
             @pl.when(gx == edge)
             def _():
@@ -429,11 +516,26 @@
                     bound = cols_old[i] + (k / 3.0) * (cols_new[i] - cols_old[i])
                     target[i, :, at] = jnp.where(lane == spot, bound, target[i, :, at])
                     return carry
-                lax.fori_loop(low, high, patch, 0)
+                lax.fori_loop(low, high, patch, 0, unroll=6)
         for edge, row in ((0, H), (tiles_y - 1, H + NYD - 1)):
             @pl.when(gy == edge)
             def _():
                 target[row] = lines[0] + (k / 3.0) * (lines[1] - lines[0])
+
+    def step(source, target, amounts, low, high, k):
+        amounts_2 = thrice(amounts)
+
+        def body(i, carry):
+            base = low + CHUNK * i
+            force = force_rows(amounts_2, row_g, col_g, base)
+            for r in range(CHUNK):
+                for t, value in enumerate(swept(source, base + r)):
+                    at = slice(128 * t, 128 * t + 128)
+                    target[base + r, :, at] = value + force[C * r : C * r + C, at]
+            return carry
+
+        lax.fori_loop(0, (high - low) // CHUNK, body, 0, unroll=True)
+        hold_edges(target, low, high, k)
 
     def gathered(source):
         wind = jnp.zeros((C, 128), F32)
@@ -453,7 +555,7 @@
         for row in rows:
             buffer[row] = jnp.zeros((C, WIDE), F32)
 
-    step(one, two, push, 1, ROWS - 1, 1)
+    finish_first()
     for move in moves:
         move.wait()
     push = thrusts(gathered(two) + missing[0], scale)
@@ -464,14 +566,6 @@
     stores = [pltpu.make_async_copy(two.at[pl.ds(H, NYD), c, pl.ds(0, NXD)], nest_out.at[c], out_sem.at[c]) for c in range(C)]
     for store in stores:
         store.start()
-
-    low_side = jnp.where(gx == 0, 0, -64)
-    high_side = jnp.where(gx == tiles_x - 1, NXD, NXD + 64)
-    fine = lax.broadcasted_iota(jnp.int32, (WIDE, 128), 0)
-    fine = jnp.where(fine < 448, fine, fine - WIDE)
-    gap = jnp.abs(fine - (3 * lanes_of((WIDE, 128)) + 1))
-    weight = jnp.where(gap <= 1, 2.0, jnp.where(gap <= 4, 1.0, 0.0))
-    weight = jnp.where((fine >= low_side) & (fine < high_side), weight, 0.0).astype(BF16)
 
     def three(m):
         y = H + 3 * m
@@ -488,7 +582,7 @@
         sum_v[C * m : C * m + C] = part[0]
         sum_v[C * (PYD + m) : C * (PYD + m) + C] = part[1]
         before, here = here, after
-    mean = jnp.dot(sum_v[...], weight, preferred_element_type=F32)
+    mean = jnp.dot(sum_v[...], weight_in[...], preferred_element_type=F32)
     half = C * PYD
     for m in range(PYD):
         i = m + PH
@@ -509,16 +603,23 @@
     smem = pl.BlockSpec(memory_space=pltpu.SMEM)
     vmem = pl.BlockSpec(memory_space=pltpu.VMEM)
     anywhere = pl.BlockSpec(memory_space=pl.ANY)
-    passed = ((NYD, C, NXD), (NEAR, C, NXD), (NEAR, C, NXD), (PYD, C, PXD), (PNEAR, C, PXD), (PNEAR, C, PXD),
-              (6, C, 128), (6, C, 128), (4, 2, C, 128), (2, C, 128), (9, C, 128))
+    passed = ((NYD, C, NXD), (NEAR, C, NXD), (NEAR, C, NXD),
+              (6, C, 128), (6, C, 128), (4, 2, C, 128), (2, C, 128), (9, C, 128),
+              (ROWS, C, WIDE), (PROWS, C, PWIDE), (ROWS, C, 128), (ROWS, C, 128), (2, C, WIDE), (ROWS, 1, 256),
+              (256, WIDE), (C, 128), (2, C, 128), (WIDE, 128))
+    halved = (14, 17)
 
     def on_device(nest_wind, parent_wind, diffusion, drift, disk_sites, disk_live, disk_coef):
         rims = pl.pallas_call(
             functools.partial(exchange, tiles_x, tiles_y),
-            out_shape=[pltpu.VMEM(shape, F32) for shape in passed],
+            out_shape=[pltpu.VMEM(shape, BF16 if i in halved else F32) for i, shape in enumerate(passed)],
             in_specs=[pl.BlockSpec(memory_space=pltpu.HBM)] * 7,
             out_specs=[vmem] * len(passed),
             scratch_shapes=[
+                pltpu.VMEM((PYD, C, PXD), F32),
+                pltpu.VMEM((PNEAR, C, PXD), F32),
+                pltpu.VMEM((PNEAR, C, PXD), F32),
+                pltpu.VMEM((PROWS, C, PWIDE), F32),
                 pltpu.VMEM((6, C, 128), F32),
                 pltpu.VMEM((6, C, 128), F32),
                 pltpu.VMEM((2, C, 128), F32),
@@ -545,13 +646,6 @@
             scratch_shapes=[
                 pltpu.VMEM((ROWS, C, WIDE), F32),
                 pltpu.VMEM((ROWS, C, WIDE), F32),
-                pltpu.VMEM((PROWS, C, PWIDE), F32),
-                pltpu.VMEM((PROWS, C, PWIDE), F32),
-                pltpu.VMEM((ROWS, C, 128), F32),
-                pltpu.VMEM((ROWS, C, 128), F32),
-                pltpu.VMEM((2, C, WIDE), F32),
-                pltpu.VMEM((ROWS, 1, 256), F32),
-                pltpu.VMEM((256, WIDE), BF16),
                 pltpu.SMEM((9, 8, 128), F32),
                 pltpu.VMEM((PYD, C, PXD), F32),
                 pltpu.VMEM((2 * C * PYD, WIDE), BF16),

time: 41.5 us -> 38.2 us (0.920)
  Pallas kernels: 40.7 us -> 37.3 us
    pallas_call x1, Pallas kernels: 11.5 us -> 8.16 us  [on_device(): pl.pallas_call(functools.partial(advance_all, tiles_x, tiles_y), out_shap...]
where the time goes in v4:
time: 38.2 us; the launch traced here: 38 us
  Pallas kernels  37.3 us (98%)
  between operations  0.67 us (2%)
    pallas_call x1, Pallas kernels, on_device(): pl.pallas_call(functools.partial(exchange, tiles_x, tiles_y), out_shape=[...  29.2 us
    pallas_call x1, Pallas kernels, on_device(): pl.pallas_call(functools.partial(advance_all, tiles_x, tiles_y), out_shap...  8.16 us

profile of v4, /device:TPU:30, one launch (start us, length us, event | category | flops | bytes accessed | tf_op | source)
XLA Modules:
  0.0 38.0 jit_solution(11607824020052134635)
XLA Ops:
  0.6 0.0 copy-start
  0.6 0.0 copy-start.1
  0.7 29.2 %exchange.1 = (f32[48,16,384]{2,1,0:T(8,128)S(1)}, f32[6,16,384]{2,1,0:T(8,128)S(1)}, f32[6,16,384]{2,1,0:T(8,128)S(1)}, f32[6,16,128]{2,1,0:T(8,128)S(1)}, f32[...) custom-call(f32[16,48,384]{2,1,0:T(8,128)} %nest.1, ...), custom_call_target="tpu_custom_call" | custom-call | tf_op jit(solution)/shard_map/exchange/pallas_call | solution.py:613
  29.8 0.0 copy-done
  29.9 0.0 copy-done.1
  29.9 8.2 %advance.1 = (f32[16,48,384]{2,1,0:T(8,128)}, f32[16,16,128]{2,1,0:T(8,128)}) custom-call(f32[16]{0:T(128)S(1)} %copy-done.1, f32[2,16]{1,0:T(2,128)S(1)} %copy-done, f32[48,16,384]{2,1,0:T(8,128)S(1)} %get-tuple-element.20.own, f32[6,16,384]{2,1,0:T(8,128)S(1)} %get-tuple-element.21.south, f32[6,16,384]{2,1,0:T(8,128)S(1)} %get-tuple-element.22.north, ...), custom_call_target="tpu_custom_call" | custom-call | tf_op jit(solution)/shard_map/advance/pallas_call | solution.py:641
Async XLA Ops:
  0.6 29.2 %copy-start = (f32[2,16]{1,0:T(2,128)S(1)}, f32[2,16]{1,0:T(2,128)}, u32[]{:S(2)}) copy-start(f32[2,16]{1,0:T(2,128)} %drift.1) | copy-start | bytes 388
  0.6 29.2 %copy-start.1 = (f32[16]{0:T(128)S(1)}, f32[16]{0:T(128)}, u32[]{:S(2)}) copy-start(f32[16]{0:T(128)} %diffusion.1) | copy-start | bytes 196

commit v5 on v4

--- a/solution.py
+++ b/solution.py
@@ -18,6 +18,8 @@
 PH = 8
 NEAR = 6
 PNEAR = 2
+NARROW = 8
+RIM = (0, 1, NYD - 2, NYD - 1)
 ROWS = NYD + 2 * H
 PROWS = PYD + 2 * PH
 WIDE = 512
@@ -104,7 +106,7 @@
 def exchange(tiles_x, tiles_y, nest, parent, diffusion_h, drift_h, sites_h, live_h, coef_h,
              own, south, north, west, east, corner, side, notes,
              two, new, cols_old, cols_new, lines, row_g, col_g, scale_out, missing_out, weight_out,
-             pown, psouth, pnorth, old, pack_w, pack_e, pack_y, own_notes, diffusion, drift, sites, live, coef, in_sem, send_sem, recv_sem):
+             pown, psouth, pnorth, old, strip_w, strip_e, pack_w, pack_e, pack_y, own_notes, diffusion, drift, sites, live, coef, in_sem, send_sem, recv_sem):
     gx, gy = lax.axis_index("gx"), lax.axis_index("gy")
 
     def device(dx, dy):
@@ -134,12 +136,19 @@
 
     lane = lanes_of((C, PXD))
     for pack, tile, first in ((pack_w, 0, 0), (pack_e, NXD // 128 - 1, 112)):
-        for p in range(NYD // 8):
+        for i, p in enumerate((0, 1, 4, 5)):
             packed = jnp.zeros((C, 128), F32)
             for j in range(8):
                 cells = own[8 * p + j, :, 128 * tile : 128 * tile + 128]
                 packed = jnp.where(lane // 16 == j, turn(cells, 16 * j - first), packed)
-            pack[p] = packed
+            pack[i] = packed
+    for strip, tile, first in ((strip_w, 0, 0), (strip_e, NXD // 128 - 1, 120)):
+        for p in range(NYD // 16):
+            packed = jnp.zeros((C, 128), F32)
+            for j in range(16):
+                cells = own[16 * p + j, :, 128 * tile : 128 * tile + 128]
+                packed = jnp.where(lane // 8 == j, turn(cells, 8 * j - first), packed)
+            strip[p] = packed
     for way, base in ((0, 0), (1, NYD - H)):
         packed = jnp.zeros((C, 128), F32)
         for i in range(H):
@@ -149,12 +158,14 @@
     strips = []
     edge = jnp.where(gy == tiles_y - 1, PYD - 1, 0)
     after = jnp.where(gy == tiles_y - 1, PYD - 2, 1)
-    for first, wide in ((0, 0), (124, 120)):
+    for first, wide, tile, beyond in ((0, 0, 0, 8), (126, 120, NXD - 128, 112)):
         packed = jnp.zeros((C, 128), F32)
         for m in range(PYD):
-            packed = jnp.where(lane // 4 == PYD + m, turn(pown[m], 64 + 4 * m - first), packed)
+            packed = jnp.where(lane // 2 == 2 * PYD + m, turn(pown[m], 64 + 2 * m - first), packed)
         packed = jnp.where(lane // 8 == 6, turn(pown[edge], 48 - wide), packed)
         packed = jnp.where(lane // 8 == 7, turn(pown[after], 56 - wide), packed)
+        for q, row in enumerate(RIM):
+            packed = jnp.where(lane // 8 == 12 + q, turn(own[row, :, tile : tile + 128], 96 + 8 * q - beyond), packed)
         strips.append(packed)
     shores = []
     for base in (0, PYD - PH):
@@ -166,7 +177,7 @@
         shores.append(packed)
 
     wide_lane = lanes_of((C, NXD))
-    inner = (wide_lane >= 4) & (wide_lane < NXD - 4)
+    inners = [(wide_lane >= n) & (wide_lane < NXD - n) for n in (4, NARROW)]
     spread = plane_tile(lambda c: diffusion[c])
     east_by = plane_tile(lambda c: drift[0, c])
     north_by = plane_tile(lambda c: drift[1, c])
@@ -182,7 +193,7 @@
     wind = jnp.zeros((C, PXD), F32)
     scale = jnp.zeros((C, PXD), F32)
     spot = jnp.zeros((C, PXD), F32)
-    rests = [jnp.zeros((C, PXD), F32)] * 2
+    rests = [jnp.zeros((C, PXD), F32)] * 3
 
     def total(value):
         return jnp.sum(value, axis=1, keepdims=True)
@@ -202,21 +213,25 @@
         square = jnp.zeros((C, NXD), F32)
         for j in range(5):
             square = jnp.where(gap == j - 2, square_weights[j], square)
-        near = {r: jnp.where(inner, own[jnp.clip(row + r, 0, NYD - 1)], 0.0) for r in range(-2, 3)}
-        along = {r: total(line * near[r]) for r in range(-1, 2)}
-        point = {r: total(jnp.where(at_0, near[r], 0.0)) for r in (-2, -1, 1, 2)}
-        ones = {0: along[0], -1: cs * point[-1], 1: cn * point[1]}
-        twos = {0: total(square * near[0]), -1: 2.0 * cs * along[-1], 1: 2.0 * cn * along[1],
-                -2: cs * cs * point[-2], 2: cn * cn * point[2]}
-        for way, (low, high) in enumerate(((NEAR, NYD - 1), (0, NYD - 1 - NEAR))):
-            for terms, at in ((ones, 4 * MAXD + s), (twos, 5 * MAXD + s)):
-                value = jnp.zeros((C, 128), F32)
-                for r, term in terms.items():
-                    value = value + term * ((row + r >= low) & (row + r <= high)).astype(F32)
-                rests[way] = jnp.where(lane == at, value, rests[way])
+        at_rim = (gy == 0) & (row == 0) | (gy == tiles_y - 1) & (row == NYD - 1)
+        second = jnp.where(at_rim, 0.0, 1.0)
+        for inner, ways in ((inners[0], ((0, NEAR, NYD - 1, 1.0), (1, 0, NYD - 1 - NEAR, 1.0))),
+                            (inners[1], ((2, 2, NYD - 3, second),))):
+            near = {r: jnp.where(inner, own[jnp.clip(row + r, 0, NYD - 1)], 0.0) for r in range(-2, 3)}
+            along = {r: total(line * near[r]) for r in range(-1, 2)}
+            point = {r: total(jnp.where(at_0, near[r], 0.0)) for r in (-2, -1, 1, 2)}
+            ones = {0: along[0], -1: cs * point[-1], 1: cn * point[1]}
+            twos = {0: total(square * near[0]), -1: 2.0 * cs * along[-1], 1: 2.0 * cn * along[1],
+                    -2: cs * cs * point[-2], 2: cn * cn * point[2]}
+            for way, low, high, kept in ways:
+                for terms, at, by in ((ones, 4 * MAXD + s, 1.0), (twos, 5 * MAXD + s, kept)):
+                    value = jnp.zeros((C, 128), F32)
+                    for r, term in terms.items():
+                        value = value + term * ((row + r >= low) & (row + r <= high)).astype(F32)
+                    rests[way] = jnp.where(lane == at, value * by, rests[way])
     mine = thrusts(wind, scale) + spot
     notes[0] = mine
-    for i, extra in enumerate((rests[0] + shores[0], rests[1] + shores[1], strips[0], strips[1])):
+    for i, extra in enumerate((rests[0] + shores[0], rests[1] + shores[1], rests[2] + strips[0], rests[2] + strips[1])):
         own_notes[i] = mine + extra
 
     for dx, dy, buffers in (
@@ -233,12 +248,12 @@
     sends += [
         (pown.at[pl.ds(PYD - PNEAR, PNEAR)], psouth, (0, 1)),
         (pown.at[pl.ds(0, PNEAR)], pnorth, (0, -1)),
-        (pack_e.at[pl.ds(4, 2)], corner.at[0], (1, 1)),
-        (pack_w.at[pl.ds(4, 2)], corner.at[1], (-1, 1)),
+        (pack_e.at[pl.ds(2, 2)], corner.at[0], (1, 1)),
+        (pack_w.at[pl.ds(2, 2)], corner.at[1], (-1, 1)),
         (pack_e.at[pl.ds(0, 2)], corner.at[2], (1, -1)),
         (pack_w.at[pl.ds(0, 2)], corner.at[3], (-1, -1)),
-        (pack_e, west, (1, 0)),
-        (pack_w, east, (-1, 0)),
+        (strip_e, west, (1, 0)),
+        (strip_w, east, (-1, 0)),
         (own.at[pl.ds(NYD - NEAR, NEAR)], south, (0, 1)),
         (own.at[pl.ds(0, NEAR)], north, (0, -1)),
         (pack_y.at[1], side.at[0], (0, 1)),
@@ -298,7 +313,7 @@
         for there in (of_x[dx], of_y[dy]):
             if there is not None:
                 first, force = first * there, force * there
-        if dx == 0 and dy != 0:
+        if (dx == 0) != (dy == 0):
             missing = [jnp.where(here, turn(note, MAXD * j - (4 + i) * MAXD), missing[i]) for i in range(2)]
         push = jnp.where(here, first, push)
         scale = jnp.where(here, force, scale)
@@ -338,7 +353,7 @@
     weight = jnp.where(gap <= 1, 2.0, jnp.where(gap <= 4, 1.0, 0.0))
     weight_out[...] = jnp.where((fine >= low_side) & (fine < high_side), weight, 0.0).astype(BF16)
 
-    for block, (source, strip_w, strip_e, base, first, count) in enumerate((
+    for block, (source, strip_w_in, strip_e_in, base, first, count) in enumerate((
         (psouth, notes[5], notes[6], 0, PH, PH),
         (pown, notes[3], notes[4], PH, 0, PYD),
         (pnorth, notes[7], notes[8], PH + PYD, 0, PH),
@@ -353,7 +368,7 @@
                 middle = source[i - (PH - PNEAR) if block == 0 else i]
             old[base + i, :, 0:128] = middle
             old[base + i, :, 128:256] = jnp.where(
-                lane < 4, turn(strip_e, -64 - 4 * m), jnp.where(lane >= 124, turn(strip_w, 60 - 4 * m), 0.0))
+                lane < 2, turn(strip_e_in, -64 - 2 * m), jnp.where(lane >= 126, turn(strip_w_in, 62 - 2 * m), 0.0))
 
     @pl.when((gy == 0) | (gy == tiles_y - 1))
     def _():
@@ -447,16 +462,22 @@
     one[H + NYD - 1, :, 0:NXD] = own[NYD - 1]
     copy_rows(north, H + NYD, NEAR)
     for p in range(ROWS // 8):
-        if p < 2:
-            from_w, from_e = corner[0, p], corner[1, p]
-        elif p < 8:
-            from_w, from_e = west[p - 2], east[p - 2]
-        else:
-            from_w, from_e = corner[2, p - 8], corner[3, p - 8]
         for j in range(8):
             y = 8 * p + j
-            one[y, :, NXD:WIDE] = jnp.where(
-                lane < 16, turn(from_e, -16 * j), jnp.where(lane >= 112, turn(from_w, 112 - 16 * j), 0.0))
+            row = y - H
+            if 0 <= row < NYD:
+                i = row % 16
+                tile = jnp.where(lane < 8, turn(east[row // 16], -8 * i),
+                                 jnp.where(lane >= 120, turn(west[row // 16], 120 - 8 * i), 0.0))
+                if row in RIM:
+                    q = RIM.index(row)
+                    tile = jnp.where(lane // 8 == 1, turn(note_in[4], -88 - 8 * q), tile)
+                    tile = jnp.where(lane // 8 == 14, turn(note_in[3], 16 - 8 * q), tile)
+            else:
+                way, i = (0, p) if y < H else (2, p - 8)
+                tile = jnp.where(lane < 16, turn(corner[way + 1, i], -16 * j),
+                                 jnp.where(lane >= 112, turn(corner[way, i], 112 - 16 * j), 0.0))
+            one[y, :, NXD:WIDE] = tile
             if y < H - NEAR or y >= H + NYD + NEAR:
                 way, i = (0, y) if y < H else (1, y - H - NYD)
                 one[y, :, 0:128] = jnp.where(lane < 4, turn(side[way], -4 * i), 0.0)
@@ -604,7 +625,7 @@
     vmem = pl.BlockSpec(memory_space=pltpu.VMEM)
     anywhere = pl.BlockSpec(memory_space=pl.ANY)
     passed = ((NYD, C, NXD), (NEAR, C, NXD), (NEAR, C, NXD),
-              (6, C, 128), (6, C, 128), (4, 2, C, 128), (2, C, 128), (9, C, 128),
+              (NYD // 16, C, 128), (NYD // 16, C, 128), (4, 2, C, 128), (2, C, 128), (9, C, 128),
               (ROWS, C, WIDE), (PROWS, C, PWIDE), (ROWS, C, 128), (ROWS, C, 128), (2, C, WIDE), (ROWS, 1, 256),
               (256, WIDE), (C, 128), (2, C, 128), (WIDE, 128))
     halved = (14, 17)
@@ -620,8 +641,10 @@
                 pltpu.VMEM((PNEAR, C, PXD), F32),
                 pltpu.VMEM((PNEAR, C, PXD), F32),
                 pltpu.VMEM((PROWS, C, PWIDE), F32),
-                pltpu.VMEM((6, C, 128), F32),
-                pltpu.VMEM((6, C, 128), F32),
+                pltpu.VMEM((NYD // 16, C, 128), F32),
+                pltpu.VMEM((NYD // 16, C, 128), F32),
+                pltpu.VMEM((4, C, 128), F32),
+                pltpu.VMEM((4, C, 128), F32),
                 pltpu.VMEM((2, C, 128), F32),
                 pltpu.VMEM((4, C, 128), F32),
                 pltpu.SMEM(diffusion.shape, F32),

time: 38.2 us -> 36.6 us (0.958)
  the two profiles are of different devices: /device:TPU:30 before, /device:TPU:24 now
where the time goes in v5:
time: 36.6 us; the launch traced here: 36.5 us
  Pallas kernels  35.8 us (98%)
  between operations  0.67 us (2%)
    pallas_call x1, Pallas kernels, on_device(): pl.pallas_call(functools.partial(exchange, tiles_x, tiles_y), out_shape=[...  27.2 us
    pallas_call x1, Pallas kernels, on_device(): pl.pallas_call(functools.partial(advance_all, tiles_x, tiles_y), out_shap...  8.62 us

profile of v5, /device:TPU:24, one launch (start us, length us, event | category | flops | bytes accessed | tf_op | source)
XLA Modules:
  0.0 36.5 jit_solution(9575458641933240027)
XLA Ops:
  0.6 0.0 copy-start
  0.6 0.0 copy-start.1
  0.7 27.2 %exchange.1 = (f32[48,16,384]{2,1,0:T(8,128)S(1)}, f32[6,16,384]{2,1,0:T(8,128)S(1)}, f32[6,16,384]{2,1,0:T(8,128)S(1)}, f32[3,16,128]{2,1,0:T(8,128)S(1)}, f32[...) custom-call(f32[16,48,384]{2,1,0:T(8,128)} %nest.1, ...), custom_call_target="tpu_custom_call" | custom-call | tf_op jit(solution)/shard_map/exchange/pallas_call | solution.py:634
  27.8 0.0 copy-done
  27.8 0.0 copy-done.1
  27.8 8.6 %advance.1 = (f32[16,48,384]{2,1,0:T(8,128)}, f32[16,16,128]{2,1,0:T(8,128)}) custom-call(f32[16]{0:T(128)S(1)} %copy-done.1, f32[2,16]{1,0:T(2,128)S(1)} %copy-done, f32[48,16,384]{2,1,0:T(8,128)S(1)} %get-tuple-element.20.own, f32[6,16,384]{2,1,0:T(8,128)S(1)} %get-tuple-element.21.south, f32[6,16,384]{2,1,0:T(8,128)S(1)} %get-tuple-element.22.north, ...), custom_call_target="tpu_custom_call" | custom-call | tf_op jit(solution)/shard_map/advance/pallas_call | solution.py:664
Async XLA Ops:
  0.6 27.2 %copy-start = (f32[2,16]{1,0:T(2,128)S(1)}, f32[2,16]{1,0:T(2,128)}, u32[]{:S(2)}) copy-start(f32[2,16]{1,0:T(2,128)} %drift.1) | copy-start | bytes 388
  0.6 27.2 %copy-start.1 = (f32[16]{0:T(128)S(1)}, f32[16]{0:T(128)}, u32[]{:S(2)}) copy-start(f32[16]{0:T(128)} %diffusion.1) | copy-start | bytes 196

commit v6 on v5

--- a/solution.py
+++ b/solution.py
@@ -507,7 +507,7 @@
                     two[y, :, at] = begun[y, :, at] + value
             return carry
 
-        lax.fori_loop(0, H - 1, frame, 0, unroll=3)
+        lax.fori_loop(0, H - 1, frame, 0, unroll=True)
 
         def inside(i, carry):
             y = H + i
@@ -521,7 +521,7 @@
                 + jnp.where(lane == 127, 0.0, ce * down) + cs * one[y - 1, :, NXD:WIDE] + cn * one[y + 1, :, NXD:WIDE])
             return carry
 
-        lax.fori_loop(0, NYD, inside, 0, unroll=6)
+        lax.fori_loop(0, NYD, inside, 0, unroll=True)
         for y, by, beyond in ((H, cs, H - 1), (H + NYD - 1, cn, H + NYD)):
             for t in range(3):
                 at = slice(128 * t, 128 * t + 128)

time: 36.6 us -> 35.7 us (0.975)
  Pallas kernels: 35.8 us -> 34.8 us
    pallas_call x1, Pallas kernels: 8.62 us -> 7.68 us  [on_device(): pl.pallas_call(functools.partial(advance_all, tiles_x, tiles_y), out_shap...]
where the time goes in v6:
time: 35.7 us; the launch traced here: 35.5 us
  Pallas kernels  34.8 us (97%)
  between operations  0.67 us (2%)
    pallas_call x1, Pallas kernels, on_device(): pl.pallas_call(functools.partial(exchange, tiles_x, tiles_y), out_shape=[...  27.2 us
    pallas_call x1, Pallas kernels, on_device(): pl.pallas_call(functools.partial(advance_all, tiles_x, tiles_y), out_shap...  7.68 us

profile of v6, /device:TPU:24, one launch (start us, length us, event | category | flops | bytes accessed | tf_op | source)
XLA Modules:
  0.0 35.5 jit_solution(10075505544507141962)
XLA Ops:
  0.6 0.0 copy-start
  0.6 0.0 copy-start.1
  0.7 27.2 %exchange.1 = (f32[48,16,384]{2,1,0:T(8,128)S(1)}, f32[6,16,384]{2,1,0:T(8,128)S(1)}, f32[6,16,384]{2,1,0:T(8,128)S(1)}, f32[3,16,128]{2,1,0:T(8,128)S(1)}, f32[...) custom-call(f32[16,48,384]{2,1,0:T(8,128)} %nest.1, ...), custom_call_target="tpu_custom_call" | custom-call | tf_op jit(solution)/shard_map/exchange/pallas_call | solution.py:634
  27.8 0.0 copy-done
  27.8 0.0 copy-done.1
  27.8 7.7 %advance.1 = (f32[16,48,384]{2,1,0:T(8,128)}, f32[16,16,128]{2,1,0:T(8,128)}) custom-call(f32[16]{0:T(128)S(1)} %copy-done.1, f32[2,16]{1,0:T(2,128)S(1)} %copy-done, f32[48,16,384]{2,1,0:T(8,128)S(1)} %get-tuple-element.20.own, f32[6,16,384]{2,1,0:T(8,128)S(1)} %get-tuple-element.21.south, f32[6,16,384]{2,1,0:T(8,128)S(1)} %get-tuple-element.22.north, ...), custom_call_target="tpu_custom_call" | custom-call | tf_op jit(solution)/shard_map/advance/pallas_call | solution.py:664
Async XLA Ops:
  0.6 27.2 %copy-start = (f32[2,16]{1,0:T(2,128)S(1)}, f32[2,16]{1,0:T(2,128)}, u32[]{:S(2)}) copy-start(f32[2,16]{1,0:T(2,128)} %drift.1) | copy-start | bytes 388
  0.6 27.2 %copy-start.1 = (f32[16]{0:T(128)S(1)}, f32[16]{0:T(128)}, u32[]{:S(2)}) copy-start(f32[16]{0:T(128)} %diffusion.1) | copy-start | bytes 196
